TPU v7x, 32 devices: a whole 2x2x4 slice. The times are simulated.
32 devices in a mesh: rcpt: 4 (over y, x), space: 8 (over z, core).
Axes of the slice: x: 2, y: 2, z: 4, core: 2. Of those that a mesh axis runs over, the one named last changes fastest.
Arguments:
- adjoint_end: float32 [32, 4, 256, 1024], P('rcpt', None, 'space'), may hold values from -6 to 6
- currents: bfloat16 [4, 2, 4, 256, 1024], P('rcpt', None, None, 'space'), may hold values from -0.29882812 to 0.29882812
- plan: int32 [4], replicated, may hold values from 0 to 3, as said below
- water_mask: int32 [256, 1024], P('space'), may hold values 0 or 1
- mixing: float32 [3, 256, 1024], P(None, 'space'), may hold values from 0.02 to 0.2
- decay: float32 [32], P('rcpt'), may hold values from 0.02 to 0.5
- obs_weight: float32 [4, 32], P(None, 'rcpt'), may hold values from 0.3 to 3
- release_cells: int32 [8, 32, 128], P('space'), may hold values from 0 to 32767
- profiles: float32 [8, 32, 512, 128], P(None, ('rcpt', 'space')), may hold values from -0.25 to 0.25
Outputs:
- adjoint_start: float32 [32, 4, 256, 1024], P('rcpt', None, 'space')
- sensitivity: float32 [8, 32, 32, 128], P(None, ('rcpt', 'space'))
Inputs may be any that keep to these rules, and one draw needn't show every extreme that they name: 4 distinct store slots; hour h's currents are currents[plan[h]], held by rcpt index plan[h].
All inputs are finite; a program needn't handle non-finite values. No bound on the sum of `water_mask` on one device may be relied on, other than what follows from the above.
Results may differ from a plain program's by a relative error of at most 0.0003.
Values may be sent and summed in bfloat16 or wider, within the bound.
A program may use at most 256 MiB of HBM per device.

v0:
```python
import jax
import jax.numpy as jnp
from jax import lax
from jax.sharding import PartitionSpec as P

HOURS = 4


diffusion_number = 0.08


def broadcast(value, axis, source):
    kept = jnp.where(lax.axis_index(axis) == source, value, 0).astype(value.dtype)
    return lax.psum(kept, axis)


def with_halo(block, sides, width):
    for axis, dim in sides:
        count = lax.axis_size(axis)
        forward = [(i, i + 1) for i in range(count - 1)]
        backward = [(target, source) for source, target in forward]
        low = lax.ppermute(
            lax.slice_in_dim(block, block.shape[dim] - width, None, axis=dim), axis, forward
        )
        high = lax.ppermute(lax.slice_in_dim(block, 0, width, axis=dim), axis, backward)
        block = jnp.concatenate([low, block, high], axis=dim)
    return block


def next_column(values):
    edge = jnp.zeros_like(values[..., :1])
    return jnp.concatenate([values[..., 1:], edge], -1)


def prev_column(values):
    edge = jnp.zeros_like(values[..., :1])
    return jnp.concatenate([edge, values[..., :-1]], -1)


def transport(extended, water, current, mixing):
    center = extended[:, :, 1:-1]
    along = current[0].astype(jnp.float32)
    across = current[1].astype(jnp.float32)
    inner = water[1:-1]
    weight_down = (jax.nn.relu(along) + diffusion_number) * water[2:]
    weight_up = (jax.nn.relu(-along) + diffusion_number) * water[:-2]
    weight_right = (jax.nn.relu(across) + diffusion_number) * next_column(inner)
    weight_left = (jax.nn.relu(-across) + diffusion_number) * prev_column(inner)
    moved = center + weight_down * (extended[:, :, 2:] - center)
    moved = moved + weight_up * (extended[:, :, :-2] - center)
    moved = moved + weight_right * (next_column(center) - center)
    moved = moved + weight_left * (prev_column(center) - center)
    moved = moved * inner
    vertical_flux = mixing * (moved[:, 1:] - moved[:, :-1])
    zeros = jnp.zeros_like(moved[:, :1])
    return (
        moved
        + jnp.concatenate([vertical_flux, zeros], 1)
        - jnp.concatenate([zeros, vertical_flux], 1)
    )


def on_device(
    adjoint_end, currents, plan, water_mask, mixing, decay, obs_weight, release_cells, profiles
):
    slot_count = currents.shape[0]
    own_rows = adjoint_end.shape[2]
    keep = (1.0 - decay)[:, None, None, None]
    hourly = []
    for hour_index in range(HOURS):
        slot_id = plan[hour_index]
        holder = slot_id // slot_count
        mine = lax.dynamic_index_in_dim(currents, slot_id % slot_count, 0, keepdims=False)
        hourly.append(broadcast(mine, "rcpt", holder))
    rim_mask = with_halo(water_mask, (("space", 0),), 1)
    water = rim_mask.astype(jnp.float32)
    inner = water[1:-1]
    source = inner * adjoint_end
    field = adjoint_end
    for hour_index in reversed(range(HOURS)):
        extended = with_halo(field, (("space", 2),), 1)
        mixed = transport(extended, water, hourly[hour_index], mixing)
        field = keep * mixed + obs_weight[hour_index][:, None, None, None] * source
    local_recv = field.shape[0]
    levels = field.shape[1]
    width = field.shape[3]
    block_count = release_cells.shape[1]
    block_cells = release_cells.shape[2]
    strip_cells = own_rows * width
    flat = field.reshape(local_recv, levels * strip_cells)
    level_start = jnp.arange(levels, dtype=jnp.int32) * strip_cells
    positions = level_start[None, :, None] + release_cells[0][:, None, :]
    picked = jnp.take(flat, positions.reshape(-1), axis=1)
    picked = picked.reshape(local_recv, block_count, levels * block_cells)
    picked = jnp.transpose(picked, (1, 0, 2))
    batches = lax.axis_size("rcpt")
    strips = lax.axis_size("space")
    sample_len = levels * block_cells
    sending = picked.reshape(1, block_count, local_recv, sample_len)
    gathered = lax.all_to_all(sending, ("rcpt", "space"), split_axis=1, concat_axis=0, tiled=True)
    own_blocks = gathered.shape[1]
    gathered = gathered.reshape(batches, strips, own_blocks, local_recv, sample_len)
    gathered = jnp.transpose(gathered, (1, 2, 0, 3, 4))
    gathered = gathered.reshape(strips, own_blocks, batches * local_recv, sample_len)
    result = jnp.einsum("sbmk,sbkp->sbmp", gathered, profiles, precision=lax.Precision.HIGHEST)
    return (field, result)


def solution(mesh):
    placed = (
        P("rcpt", None, "space", None),
        P("rcpt", None, None, "space", None),
        P(),
        P("space", None),
        P(None, "space", None),
        P("rcpt"),
        P(None, "rcpt"),
        P("space", None, None),
        P(None, ("rcpt", "space"), None, None),
    )
    return jax.shard_map(
        on_device,
        mesh=mesh,
        in_specs=placed,
        out_specs=(P("rcpt", None, "space", None), P(None, ("rcpt", "space"), None, None)),
        check_vma=False,
    )
```

profile of v0, /device:TPU:0, one launch (start us, length us, event | category | flops | bytes accessed | tf_op | source)
XLA Modules:
  0.0 507.4 jit_solution(16071324985046801121)
XLA Ops:
  7.2 0.0 copy-start
  7.2 0.0 all-reduce.21.cloned.1.call-start
  7.2 0.9 fusion.113
  8.1 2.3 collective-permute-start
  10.5 0.0 copy-start.21
  10.5 0.0 copy-start.16
  10.5 1.4 collective-permute-start.1
  12.0 4.6 copy.20
  16.6 0.0 copy-start.2
  16.6 2.0 copy-done.2
  18.6 1.3 collective-permute-start.2
  19.9 6.4 %collective-permute-start.3 = (f32[8,4,1,1024]{3,0,2,1:T(8,128)S(1)}, f32[8,4,1,1024]{3,0,2,1:T(8,128)S(1)}, u32[]{:S(2)}, u32[]{:S(2)}) collective-permute-start(f32[8,4,1,1024]{3,0,2,1:T(8,128)S(1)} %get-tuple-element.27), channel_id=1, source_target_pairs={{0,1},{1,2},{2,3},{3,4},{4,5},{5,6},{6,7},{8,9},{9,10},{10,11},{11... | collective-permute-start | bytes 393224 | tf_op jit(solution)/shard_map/ppermute | solution.py:22
  26.4 0.7 fusion.114
  29.6 1.4 select_bitcast_fusion.1
  31.0 0.0 all-reduce.21.cloned.1.call-update
  31.1 0.5 slice_bitcast_fusion
  31.6 0.1 broadcast_add_fusion
  31.7 0.1 compare_select_fusion
  31.8 0.1 broadcast_bitcast_fusion
  31.9 0.6 broadcast_clamp_fusion
  32.5 8.2 %fusion.109 = (f32[8,4,32,1023]{3,0,2,1:T(8,128)}, f32[8,4,32,1023]{3,0,2,1:T(8,128)}) fusion(f32[8,4,32,1024]{3,0,2,1:T(8,128)} %copy-done.2), kind=kLoop, calls=%fused_computation.159 | loop fusion | bytes 16760832 | tf_op jit(solution)/shard_map/slice | solution.py:32
  40.7 0.5 broadcast_subtract_fusion
  41.2 0.0 collective-permute-done
  41.2 0.0 collective-permute-done.1
  41.3 0.1 fusion.112
  41.4 0.1 concatenate.96
  41.5 0.0 copy-start.11
  41.5 61.7 %all-reduce.21.cloned.1.call-done = (bf16[2,4,32,1024]{3,2,1,0:T(8,128)(2,1)}, bf16[2,4,32,1024]{3,2,1,0:T(8,128)(2,1)}, bf16[2,4,32,1024]{3,2,1,0:T(8,128)(2,1)}, bf16[2,4,32,1024]{3,2,1,0:T(8,128)(2,1)}) async-done(((bf16[2,4,32,1024]{3,2,1,0:T(8,128)(2,1)}, bf16[2,4,32,1024]{3,2,1,0:T(8,128)(2,1)}, bf16[2,4,32,1024]{3,2,1,0:T(8,128)(2,1)}, bf16[2,4,32,1024]{3,2,1,0:T(8,128)(2,1)}), ...) | async-done | bytes 2097168 | tf_op jit(solution)/shard_map/psum | solution.py:14
  103.2 1.3 fusion.47
  104.5 0.0 collective-permute-done.3
  104.5 0.0 copy-start.3
  104.5 9.7 %fusion.32 = f32[8,4,32,1024]{3,0,2,1:T(8,128)S(1)} fusion(f32[8,4,32,1024]{3,0,2,1:T(8,128)} %copy-done.2, f32[8,4,1,1024]{3,0,2,1:T(8,128)S(1)} %collective-permute-done.3, f32[8,4,1,1024]{3,0,2,1:T(8,128)S(1)} %collective-permute-done.2, f32[8,4,32,1023]{3,0,2,1:T(8,128)} %get-tuple-element.25, f32[8,4,32,1023]{3,0,2,1:T(8,128)} %get-tuple-element.24, ...), kind=kLoop, calls=%fused_computation.40 | loop fusion | flops 15728640 | bytes 19259392 | tf_op jit(solution)/shard_map/mul | solution.py:53
  114.2 0.0 copy-start.1
  114.3 2.3 fusion.39
  116.6 1.0 copy-done.1
  117.6 6.5 %multiply_add_fusion.3 = f32[8,4,32,1024]{3,0,2,1:T(8,128)S(1)} fusion(f32[8,3,32,1024]{3,0,2,1:T(8,128)} %fusion.39, f32[8,4,32,1024]{3,0,2,1:T(8,128)S(1)} %fusion.32, f32[8]{0:T(128)S(1)} %copy-done.25, f32[32,1024]{1,0:T(8,128)S(1)} %get-tuple-element.61, f32[8]{0:T(128)S(1)} %copy-done.20, f32[8,4,32,1024]{3,2,1,0:T(8,128)S(1)} %copy-done.1), kind=kLoop, calls=%fused_computation.48 | loop fusion | flops 6291456 | bytes 15859776 | tf_op jit(solution)/shard_map/add | solution.py:83
  124.1 0.0 copy-start.12
  124.1 4.9 fusion.107
  129.0 1.3 collective-permute-start.4
  130.3 3.2 collective-permute-start.5
  133.6 2.3 fusion.61
  135.9 7.1 %fusion.23 = f32[8,4,32,1024]{3,0,2,1:T(8,128)S(1)} fusion(f32[8,4,32,1024]{3,0,2,1:T(8,128)S(1)} %multiply_add_fusion.3, f32[8,4,1,1024]{3,0,2,1:T(8,128)S(1)} %collective-permute-done.5, f32[8,4,1,1024]{3,0,2,1:T(8,128)S(1)} %collective-permute-done.4, f32[8,4,32,1023]{3,0,2,1:T(8,128)} %get-tuple-element.21, f32[8,4,32,1023]{3,0,2,1:T(8,128)} %get-tuple-element.20, ...), kind=kLoop, calls=%fused_computation.29 | loop fusion | flops 15728640 | bytes 19259392 | tf_op jit(solution)/shard_map/mul | solution.py:53
  143.1 2.3 fusion.38
  145.4 6.5 %multiply_add_fusion.2 = f32[8,4,32,1024]{3,0,2,1:T(8,128)S(1)} fusion(f32[8,3,32,1024]{3,0,2,1:T(8,128)} %fusion.38, f32[8,4,32,1024]{3,0,2,1:T(8,128)S(1)} %fusion.23, f32[8]{0:T(128)S(1)} %copy-done.24, f32[32,1024]{1,0:T(8,128)S(1)} %get-tuple-element.61, f32[8]{0:T(128)S(1)} %copy-done.20, f32[8,4,32,1024]{3,2,1,0:T(8,128)S(1)} %copy-done.1), kind=kLoop, calls=%fused_computation.47 | loop fusion | flops 6291456 | bytes 15859776 | tf_op jit(solution)/shard_map/add | solution.py:83
  151.9 1.3 collective-permute-start.6
  153.3 4.0 collective-permute-start.7
  157.3 4.9 fusion.105
  162.2 7.2 %fusion.14 = f32[8,4,32,1024]{3,0,2,1:T(8,128)S(1)} fusion(f32[8,4,32,1024]{3,0,2,1:T(8,128)S(1)} %multiply_add_fusion.2, f32[8,4,1,1024]{3,0,2,1:T(8,128)S(1)} %collective-permute-done.7, f32[8,4,1,1024]{3,0,2,1:T(8,128)S(1)} %collective-permute-done.6, f32[8,4,32,1023]{3,0,2,1:T(8,128)} %get-tuple-element.17, f32[8,4,32,1023]{3,0,2,1:T(8,128)} %get-tuple-element.16, ...), kind=kLoop, calls=%fused_computation.18 | loop fusion | flops 15728640 | bytes 19259392 | tf_op jit(solution)/shard_map/mul | solution.py:53
  169.4 2.3 fusion.37
  171.7 6.5 %multiply_add_fusion.1 = f32[8,4,32,1024]{3,0,2,1:T(8,128)S(1)} fusion(f32[8,3,32,1024]{3,0,2,1:T(8,128)} %fusion.37, f32[8,4,32,1024]{3,0,2,1:T(8,128)S(1)} %fusion.14, f32[8]{0:T(128)S(1)} %copy-done.23, f32[32,1024]{1,0:T(8,128)S(1)} %get-tuple-element.61, f32[8]{0:T(128)S(1)} %copy-done.20, f32[8,4,32,1024]{3,2,1,0:T(8,128)S(1)} %copy-done.1), kind=kLoop, calls=%fused_computation.46 | loop fusion | flops 6291456 | bytes 15859776 | tf_op jit(solution)/shard_map/add | solution.py:83
  178.3 1.3 collective-permute-start.8
  179.6 4.7 collective-permute-start.9
  184.3 4.9 fusion.103
  189.3 7.1 %fusion.5 = f32[8,4,32,1024]{3,0,2,1:T(8,128)S(1)} fusion(f32[8,4,32,1024]{3,0,2,1:T(8,128)S(1)} %multiply_add_fusion.1, f32[8,4,1,1024]{3,0,2,1:T(8,128)S(1)} %collective-permute-done.9, f32[8,4,1,1024]{3,0,2,1:T(8,128)S(1)} %collective-permute-done.8, f32[8,4,32,1023]{3,0,2,1:T(8,128)} %get-tuple-element.13, f32[8,4,32,1023]{3,0,2,1:T(8,128)} %get-tuple-element.12, ...), kind=kLoop, calls=%fused_computation.7 | loop fusion | flops 15728640 | bytes 19259392 | tf_op jit(solution)/shard_map/mul | solution.py:53
  196.4 0.8 fusion.36
  197.3 5.4 %multiply_add_fusion = f32[8,4,32,1024]{3,0,2,1:T(8,128)} fusion(f32[8,3,32,1024]{3,0,2,1:T(8,128)S(1)} %fusion.36, f32[8,4,32,1024]{3,0,2,1:T(8,128)S(1)} %fusion.5, f32[8]{0:T(128)S(1)} %copy-done.22, f32[32,1024]{1,0:T(8,128)S(1)} %get-tuple-element.61, f32[8]{0:T(128)S(1)} %copy-done.20, f32[8,4,32,1024]{3,2,1,0:T(8,128)S(1)} %copy-done.1), kind=kLoop, calls=%fused_computation.45 | loop fusion | flops 6291456 | bytes 15859776 | tf_op jit(solution)/shard_map/add | solution.py:83
  202.7 30.4 %copy.29 = f32[8,4,32,1024]{0,3,2,1:T(8,128)} copy(f32[8,4,32,1024]{3,0,2,1:T(8,128)} %multiply_add_fusion) | data formatting | bytes 8388608 | tf_op jit(solution)/shard_map/add | solution.py:83
  233.1 237.6 %gather_fusion = f32[16384,8]{1,0:T(8,128)} fusion(f32[8,131072]{0,1:T(8,128)} %bitcast.30, s32[16384]{0:T(1024)S(1)} %copy-done.17), kind=kCustom, calls=%fused_computation | custom fusion | bytes 1114112 | tf_op jit(solution)/shard_map/jit(_take)/gather | solution.py:93
  470.7 5.2 %copy.30 = f32[8,32,512]{2,0,1:T(8,128)S(1)} copy(f32[8,32,512]{0,2,1:T(8,128)} %bitcast.87) | data formatting | bytes 1048576 | tf_op jit(solution)/shard_map/jit(_take)/gather | solution.py:93
  475.9 0.9 select_bitcast_fusion
  476.8 5.3 %all-to-all-start = ((f32[1,32,8,512]{3,2,0,1:T(8,128)}), f32[1,32,8,512]{3,2,0,1:T(8,128)S(1)}, u32[]{:S(2)}, u32[]{:S(2)}) async-start(f32[1,32,8,512]{3,2,0,1:T(8,128)} %select_bitcast_fusion), calls=%async_computation | async-start | bytes 1048576 | tf_op jit(solution)/shard_map/all_to_all | solution.py:100
  482.1 6.6 %copy.32 = f32[8,4,32,1024]{3,2,1,0:T(8,128)} copy(f32[8,4,32,1024]{3,0,2,1:T(8,128)} %multiply_add_fusion) | data formatting | bytes 8388608
  488.7 9.7 %all-to-all-done = f32[1,32,8,512]{3,2,0,1:T(8,128)S(1)} async-done(((f32[1,32,8,512]{3,2,0,1:T(8,128)}), f32[1,32,8,512]{3,2,0,1:T(8,128)S(1)}, u32[]{:S(2)}, u32[]{:S(2)}) %all-to-all-start) | async-done | bytes 524320 | tf_op jit(solution)/shard_map/all_to_all | solution.py:100
  498.4 1.9 fusion.42
  (63 shorter events, 0.3 us)
Async XLA Ops:
  7.2 491.2 %copy-start = (f32[8,1,512,128]{3,2,1,0:T(8,128)S(1)}, f32[8,1,512,128]{3,2,1,0:T(8,128)}, u32[]{:S(2)}) copy-start(f32[8,1,512,128]{3,2,1,0:T(8,128)} %param.17) | copy-start | bytes 6291460
  7.2 96.0 %all-reduce.21.cloned.1.call-start = ((), (), s32[]{:S(2)}) async-start(), calls=%async_computation.1 | async-start | bytes 4194304 | tf_op jit(solution)/shard_map/psum | solution.py:14
  8.1 33.1 %collective-permute-start = (s32[1,1024]{1,0:T(1,128)S(1)}, s32[1,1024]{1,0:T(1,128)S(1)}, u32[]{:S(2)}, u32[]{:S(2)}) collective-permute-start(s32[1,1024]{1,0:T(1,128)S(1)} %get-tuple-element.65), channel_id=1, source_target_pairs={{0,1},{1,2},{2,3},{3,4},{4,5},{5,6},{6,7},{8,9},{9,10},{10,11},{11... | collective-permute-start | bytes 12296 | tf_op jit(solution)/shard_map/ppermute | solution.py:22
  10.5 15.9 %copy-start.21 = (s32[4]{0:T(128)S(1)}, s32[4]{0:T(128)}, u32[]{:S(2)}) copy-start(s32[4]{0:T(128)} %param.11) | copy-start | bytes 52
  10.5 19.0 %copy-start.16 = (bf16[1,2,4,32,1024]{4,3,2,1,0:T(8,128)(2,1)S(1)}, bf16[1,2,4,32,1024]{4,3,2,1,0:T(8,128)(2,1)}, u32[]{:S(2)}) copy-start(bf16[1,2,4,32,1024]{4,3,2,1,0:T(8,128)(2,1)} %param.10) | copy-start | bytes 1572868
  10.5 30.7 %collective-permute-start.1 = (s32[1,1024]{1,0:T(1,128)S(1)}, s32[1,1024]{1,0:T(1,128)S(1)}, u32[]{:S(2)}, u32[]{:S(2)}) collective-permute-start(s32[1,1024]{1,0:T(1,128)S(1)} %get-tuple-element.66), channel_id=1, source_target_pairs={{1,0},{2,1},{3,2},{4,3},{5,4},{6,5},{7,6},{9,8},{10,9},{11,10},{12... | collective-permute-start | bytes 12296 | tf_op jit(solution)/shard_map/ppermute | solution.py:25
  16.6 2.0 copy-start.2
  18.6 12.5 %copy-start.26 = (f32[4,8]{1,0:T(4,128)S(1)}, f32[4,8]{1,0:T(4,128)}, u32[]{:S(2)}) copy-start(f32[4,8]{1,0:T(4,128)} %param.15) | copy-start | bytes 388
  18.6 13.0 %copy-start.19 = (s32[1,32,128]{2,1,0:T(8,128)S(1)}, s32[1,32,128]{2,1,0:T(8,128)}, u32[]{:S(2)}) copy-start(s32[1,32,128]{2,1,0:T(8,128)} %param.16) | copy-start | bytes 49156
  18.6 85.9 %collective-permute-start.2 = (f32[8,4,1,1024]{3,0,2,1:T(8,128)S(1)}, f32[8,4,1,1024]{3,0,2,1:T(8,128)S(1)}, u32[]{:S(2)}, u32[]{:S(2)}) collective-permute-start(f32[8,4,1,1024]{3,0,2,1:T(8,128)S(1)} %get-tuple-element.26), channel_id=1, source_target_pairs={{1,0},{2,1},{3,2},{4,3},{5,4},{6,5},{7,6},{9,8},{10,9},{11,10},{12... | collective-permute-start | bytes 393224 | tf_op jit(solution)/shard_map/ppermute | solution.py:25
  19.9 84.6 %collective-permute-start.3 = (f32[8,4,1,1024]{3,0,2,1:T(8,128)S(1)}, f32[8,4,1,1024]{3,0,2,1:T(8,128)S(1)}, u32[]{:S(2)}, u32[]{:S(2)}) collective-permute-start(f32[8,4,1,1024]{3,0,2,1:T(8,128)S(1)} %get-tuple-element.27), channel_id=1, source_target_pairs={{0,1},{1,2},{2,3},{3,4},{4,5},{5,6},{6,7},{8,9},{9,10},{10,11},{11... | collective-permute-start | bytes 393224 | tf_op jit(solution)/shard_map/ppermute | solution.py:22
  32.5 8.2 %copy-start.27 = (f32[8]{0:T(128)S(1)}, f32[8]{0:T(128)}, u32[]{:S(2)}) copy-start(f32[8]{0:T(128)} %param.14) | copy-start | bytes 100
  32.5 8.7 %copy-start.18 = (s32[32,1024]{1,0:T(8,128)S(1)}, s32[32,1024]{1,0:T(8,128)}, u32[]{:S(2)}) copy-start(s32[32,1024]{1,0:T(8,128)} %param.12) | copy-start | bytes 393220
  41.5 63.0 %copy-start.11 = (f32[32,1024]{1,0:T(8,128)}, f32[32,1024]{1,0:T(8,128)S(1)}, u32[]{:S(2)}) copy-start(f32[32,1024]{1,0:T(8,128)S(1)} %get-tuple-element.62) | copy-start | bytes 393220
  104.5 9.7 %copy-start.3 = (f32[3,32,1024]{2,1,0:T(8,128)S(1)}, f32[3,32,1024]{2,1,0:T(8,128)}, u32[]{:S(2)}) copy-start(f32[3,32,1024]{2,1,0:T(8,128)} %param.13) | copy-start | bytes 1179652
  114.2 3.3 copy-start.1
  114.2 3.3 copy-start.20
  114.2 3.3 copy-start.25
  124.1 9.5 %copy-start.12 = (f32[32,1024]{1,0:T(8,128)S(1)}, f32[32,1024]{1,0:T(8,128)}, u32[]{:S(2)}) copy-start(f32[32,1024]{1,0:T(8,128)} %copy-done.11) | copy-start | bytes 393220
  124.1 9.5 %copy-start.13 = (bf16[2,4,32,1024]{3,2,1,0:T(8,128)(2,1)S(1)}, bf16[2,4,32,1024]{3,2,1,0:T(8,128)(2,1)}, u32[]{:S(2)}) copy-start(bf16[2,4,32,1024]{3,2,1,0:T(8,128)(2,1)} %get-tuple-element.9) | copy-start | bytes 1572868
  124.1 9.5 %copy-start.14 = (bf16[2,4,32,1024]{3,2,1,0:T(8,128)(2,1)S(1)}, bf16[2,4,32,1024]{3,2,1,0:T(8,128)(2,1)}, u32[]{:S(2)}) copy-start(bf16[2,4,32,1024]{3,2,1,0:T(8,128)(2,1)} %get-tuple-element.10) | copy-start | bytes 1572868
  124.1 9.5 %copy-start.15 = (bf16[2,4,32,1024]{3,2,1,0:T(8,128)(2,1)S(1)}, bf16[2,4,32,1024]{3,2,1,0:T(8,128)(2,1)}, u32[]{:S(2)}) copy-start(bf16[2,4,32,1024]{3,2,1,0:T(8,128)(2,1)} %get-tuple-element.11) | copy-start | bytes 1572868
  129.0 6.9 %collective-permute-start.4 = (f32[8,4,1,1024]{3,0,2,1:T(8,128)S(1)}, f32[8,4,1,1024]{3,0,2,1:T(8,128)S(1)}, u32[]{:S(2)}, u32[]{:S(2)}) collective-permute-start(f32[8,4,1,1024]{3,0,2,1:T(8,128)S(1)} %get-tuple-element.22), channel_id=1, source_target_pairs={{1,0},{2,1},{3,2},{4,3},{5,4},{6,5},{7,6},{9,8},{10,9},{11,10},{12... | collective-permute-start | bytes 393224 | tf_op jit(solution)/shard_map/ppermute | solution.py:25
  130.3 5.6 %collective-permute-start.5 = (f32[8,4,1,1024]{3,0,2,1:T(8,128)S(1)}, f32[8,4,1,1024]{3,0,2,1:T(8,128)S(1)}, u32[]{:S(2)}, u32[]{:S(2)}) collective-permute-start(f32[8,4,1,1024]{3,0,2,1:T(8,128)S(1)} %get-tuple-element.23), channel_id=1, source_target_pairs={{0,1},{1,2},{2,3},{3,4},{4,5},{5,6},{6,7},{8,9},{9,10},{10,11},{11... | collective-permute-start | bytes 393224 | tf_op jit(solution)/shard_map/ppermute | solution.py:22
  143.1 2.3 copy-start.24
  151.9 10.2 %collective-permute-start.6 = (f32[8,4,1,1024]{3,0,2,1:T(8,128)S(1)}, f32[8,4,1,1024]{3,0,2,1:T(8,128)S(1)}, u32[]{:S(2)}, u32[]{:S(2)}) collective-permute-start(f32[8,4,1,1024]{3,0,2,1:T(8,128)S(1)} %get-tuple-element.18), channel_id=1, source_target_pairs={{1,0},{2,1},{3,2},{4,3},{5,4},{6,5},{7,6},{9,8},{10,9},{11,10},{12... | collective-permute-start | bytes 393224 | tf_op jit(solution)/shard_map/ppermute | solution.py:25
  153.2 9.0 %copy-start.7 = (f32[4,32,1024]{2,1,0:T(8,128)S(1)}, f32[4,32,1024]{2,1,0:T(8,128)}, u32[]{:S(2)}) copy-start(f32[4,32,1024]{2,1,0:T(8,128)} %get-tuple-element.48) | copy-start | bytes 1572868
  153.2 8.9 %copy-start.8 = (f32[4,32,1024]{2,1,0:T(8,128)S(1)}, f32[4,32,1024]{2,1,0:T(8,128)}, u32[]{:S(2)}) copy-start(f32[4,32,1024]{2,1,0:T(8,128)} %get-tuple-element.49) | copy-start | bytes 1572868
  153.3 8.9 %copy-start.9 = (f32[4,32,1024]{2,1,0:T(8,128)S(1)}, f32[4,32,1024]{2,1,0:T(8,128)}, u32[]{:S(2)}) copy-start(f32[4,32,1024]{2,1,0:T(8,128)} %get-tuple-element.50) | copy-start | bytes 1572868
  153.3 8.9 %copy-start.10 = (f32[4,32,1024]{2,1,0:T(8,128)S(1)}, f32[4,32,1024]{2,1,0:T(8,128)}, u32[]{:S(2)}) copy-start(f32[4,32,1024]{2,1,0:T(8,128)} %get-tuple-element.51) | copy-start | bytes 1572868
  153.3 8.9 %collective-permute-start.7 = (f32[8,4,1,1024]{3,0,2,1:T(8,128)S(1)}, f32[8,4,1,1024]{3,0,2,1:T(8,128)S(1)}, u32[]{:S(2)}, u32[]{:S(2)}) collective-permute-start(f32[8,4,1,1024]{3,0,2,1:T(8,128)S(1)} %get-tuple-element.19), channel_id=1, source_target_pairs={{0,1},{1,2},{2,3},{3,4},{4,5},{5,6},{6,7},{8,9},{9,10},{10,11},{11... | collective-permute-start | bytes 393224 | tf_op jit(solution)/shard_map/ppermute | solution.py:22
  169.4 2.3 copy-start.23
  178.3 11.0 %collective-permute-start.8 = (f32[8,4,1,1024]{3,0,2,1:T(8,128)S(1)}, f32[8,4,1,1024]{3,0,2,1:T(8,128)S(1)}, u32[]{:S(2)}, u32[]{:S(2)}) collective-permute-start(f32[8,4,1,1024]{3,0,2,1:T(8,128)S(1)} %get-tuple-element.14), channel_id=1, source_target_pairs={{1,0},{2,1},{3,2},{4,3},{5,4},{6,5},{7,6},{9,8},{10,9},{11,10},{12... | collective-permute-start | bytes 393224 | tf_op jit(solution)/shard_map/ppermute | solution.py:25
  179.6 9.7 %copy-start.4 = (f32[4,32,1024]{2,1,0:T(8,128)S(1)}, f32[4,32,1024]{2,1,0:T(8,128)}, u32[]{:S(2)}) copy-start(f32[4,32,1024]{2,1,0:T(8,128)} %get-tuple-element.45) | copy-start | bytes 1572868
  179.6 9.7 %copy-start.5 = (f32[4,32,1024]{2,1,0:T(8,128)S(1)}, f32[4,32,1024]{2,1,0:T(8,128)}, u32[]{:S(2)}) copy-start(f32[4,32,1024]{2,1,0:T(8,128)} %get-tuple-element.46) | copy-start | bytes 1572868
  179.6 9.7 %copy-start.6 = (f32[4,32,1024]{2,1,0:T(8,128)S(1)}, f32[4,32,1024]{2,1,0:T(8,128)}, u32[]{:S(2)}) copy-start(f32[4,32,1024]{2,1,0:T(8,128)} %get-tuple-element.47) | copy-start | bytes 1572868
  179.6 9.7 %collective-permute-start.9 = (f32[8,4,1,1024]{3,0,2,1:T(8,128)S(1)}, f32[8,4,1,1024]{3,0,2,1:T(8,128)S(1)}, u32[]{:S(2)}, u32[]{:S(2)}) collective-permute-start(f32[8,4,1,1024]{3,0,2,1:T(8,128)S(1)} %get-tuple-element.15), channel_id=1, source_target_pairs={{0,1},{1,2},{2,3},{3,4},{4,5},{5,6},{6,7},{8,9},{9,10},{10,11},{11... | collective-permute-start | bytes 393224 | tf_op jit(solution)/shard_map/ppermute | solution.py:22
  196.4 0.8 copy-start.22
  202.7 30.4 %copy-start.17 = (s32[16384]{0:T(1024)S(1)}, s32[16384]{0:T(1024)}, u32[]{:S(2)}) copy-start(s32[16384]{0:T(1024)} %broadcast_clamp_fusion) | copy-start | bytes 196612
  476.8 21.6 %all-to-all-start = ((f32[1,32,8,512]{3,2,0,1:T(8,128)}), f32[1,32,8,512]{3,2,0,1:T(8,128)S(1)}, u32[]{:S(2)}, u32[]{:S(2)}) async-start(f32[1,32,8,512]{3,2,0,1:T(8,128)} %select_bitcast_fusion), calls=%async_computation | async-start | bytes 1048576 | tf_op jit(solution)/shard_map/all_to_all | solution.py:100
Sparse Core Ops, SparseCore 0:
  31.2 71.9 all-reduce.20
where the time goes:
time: 513 us; the launch traced here: 507 us
  local copies, waits for them, and re-layouts  313 us (61%)
  waiting for transfers between devices  71.4 us (14%)
  other arithmetic  71.1 us (14%)
  starting transfers between devices  32.6 us (6%)
  between operations  17.5 us (3%)
    gather x2, local copies, waits for them, and re-layouts, on_device(): picked = jnp.take(flat, positions.reshape(-1), axis=1)  243 us
    psum x1, waiting for transfers between devices, broadcast(): return lax.psum(kept, axis)  61.7 us
    mul x4, other arithmetic, transport(): moved = moved * inner  31.1 us
    add x1, local copies, waits for them, and re-layouts, on_device(): field = keep * mixed + obs_weight[hour_index][:, None, None, None] * source  30.4 us
    add x4, other arithmetic, on_device(): field = keep * mixed + obs_weight[hour_index][:, None, None, None] * source  24.9 us
    slice x5, local copies, waits for them, and re-layouts, next_column(): return jnp.concatenate([values[..., 1:], edge], -1)  23 us
    ppermute x5, starting transfers between devices, with_halo(): lax.ppermute(lax.slice_in_dim(block, block.shape[dim] - width, None, axis...  20.7 us
    unnamed x58, local copies, waits for them, and re-layouts  14.3 us
  transfers between devices with their start and end apart: 12, of which 2 were waited for; matrix products, arithmetic and copies ran while one was open for 7% of the time, Pallas kernels for 0%

commit v1 on v0

v1 whole, which is shorter than its diff:
```python
import functools

import jax
import jax.numpy as jnp
from jax import lax
from jax.experimental import pallas as pl
from jax.experimental.pallas import tpu as pltpu
from jax.sharding import PartitionSpec as P

HOURS = 4
LANES = 128
SUBROWS = 16
MESH = pl.DeviceIdType.MESH
VMEM_LIMIT = 48 * 1024 * 1024

diffusion_number = 0.08


def steps_kernel(
    batches, strips,
    plan_ref, decay_ref, obs_ref, water_ref, mix_ref, adj_hbm, cur_hbm,
    out_hbm,
    cur_buf, raw, fa, fb, src, halo, water_halo, gate, weight,
    cur_send, cur_recv, cur_own, halo_send, halo_recv, wat_send, wat_recv, in_sem, out_sem,
):
    recv, levels, rows, width = adj_hbm.shape
    slots = cur_hbm.shape[0]
    me = lax.axis_index("rcpt")
    strip = lax.axis_index("space")
    has_up = strip > 0
    has_down = strip < strips - 1

    barrier = pltpu.get_barrier_semaphore()
    for d in range(1, batches):
        pl.semaphore_signal(
            barrier, inc=1, device_id={"rcpt": lax.rem(me + d, batches)}, device_id_type=MESH
        )

    @pl.when(has_up)
    def _():
        pl.semaphore_signal(barrier, inc=1, device_id={"space": strip - 1}, device_id_type=MESH)

    @pl.when(has_down)
    def _():
        pl.semaphore_signal(barrier, inc=1, device_id={"space": strip + 1}, device_id_type=MESH)

    loads = [
        pltpu.make_async_copy(adj_hbm.at[r], raw.at[r], in_sem.at[r]) for r in range(recv)
    ]
    for load in loads:
        load.start()
    own_slots = cur_buf.at[pl.ds(me * slots, slots)]
    own_copy = pltpu.make_async_copy(cur_hbm, own_slots, cur_own)
    own_copy.start()

    peers = batches - 1 + has_up.astype(jnp.int32) + has_down.astype(jnp.int32)
    pl.semaphore_wait(barrier, peers)

    spread = []
    for d in range(1, batches):
        copy = pltpu.make_async_remote_copy(
            src_ref=cur_hbm, dst_ref=own_slots,
            send_sem=cur_send.at[d - 1], recv_sem=cur_recv.at[d - 1],
            device_id={"rcpt": lax.rem(me + d, batches)}, device_id_type=MESH,
        )
        copy.start()
        spread.append(copy)

    def water_copies():
        up = pltpu.make_async_remote_copy(
            src_ref=water_ref.at[pl.ds(0, 8)], dst_ref=water_halo.at[1],
            send_sem=wat_send.at[0], recv_sem=wat_recv.at[0],
            device_id={"space": strip - 1}, device_id_type=MESH,
        )
        down = pltpu.make_async_remote_copy(
            src_ref=water_ref.at[pl.ds(rows - 8, 8)], dst_ref=water_halo.at[0],
            send_sem=wat_send.at[1], recv_sem=wat_recv.at[1],
            device_id={"space": strip + 1}, device_id_type=MESH,
        )
        return up, down

    def halo_copies(step, field):
        up = pltpu.make_async_remote_copy(
            src_ref=field.at[:, 0], dst_ref=halo.at[step, 1],
            send_sem=halo_send.at[step, 0], recv_sem=halo_recv.at[step, 0],
            device_id={"space": strip - 1}, device_id_type=MESH,
        )
        down = pltpu.make_async_remote_copy(
            src_ref=field.at[:, rows - 1], dst_ref=halo.at[step, 0],
            send_sem=halo_send.at[step, 1], recv_sem=halo_recv.at[step, 1],
            device_id={"space": strip + 1}, device_id_type=MESH,
        )
        return up, down

    def start(copies):
        up, down = copies

        @pl.when(has_up)
        def _():
            up.start()

        @pl.when(has_down)
        def _():
            down.start()

    def finish(copies):
        up, down = copies

        @pl.when(has_up)
        def _():
            up.wait_send()
            down.wait_recv()

        @pl.when(has_down)
        def _():
            down.wait_send()
            up.wait_recv()

    water_pair = water_copies()
    start(water_pair)

    for load in loads:
        load.wait()

    def arrange(t, _):
        for level in range(levels):
            block = raw[:, level, pl.ds(pl.multiple_of(t * 8, 8), 8), :]
            fa[level, pl.ds(t * 8, 8)] = jnp.swapaxes(block, 0, 1)
        return 0

    lax.fori_loop(0, rows // 8, arrange, 0)
    pair = halo_copies(0, fa)
    start(pair)

    @pl.when(jnp.logical_not(has_up))
    def _():
        water_halo[0] = jnp.zeros_like(water_halo[0])
        for step in range(HOURS):
            halo[step, 0] = jnp.zeros_like(halo[step, 0])

    @pl.when(jnp.logical_not(has_down))
    def _():
        water_halo[1] = jnp.zeros_like(water_halo[1])
        for step in range(HOURS):
            halo[step, 1] = jnp.zeros_like(halo[step, 1])

    finish(water_pair)
    inner = water_ref[...].astype(jnp.float32)
    above = water_halo[0, 7:8, :].astype(jnp.float32)
    below = water_halo[1, 0:1, :].astype(jnp.float32)
    row_at = lax.broadcasted_iota(jnp.int32, (rows, width), 0)
    col_at = lax.broadcasted_iota(jnp.int32, (rows, width), 1)
    up_water = jnp.where(row_at == 0, above, pltpu.roll(inner, 1, 0))
    down_water = jnp.where(row_at == rows - 1, below, pltpu.roll(inner, rows - 1, 0))
    left_water = jnp.where(col_at == 0, 0.0, pltpu.roll(inner, 1, 1))
    right_water = jnp.where(col_at == width - 1, 0.0, pltpu.roll(inner, width - 1, 1))
    gate[0] = inner
    gate[1] = inner * up_water
    gate[2] = inner * down_water
    gate[3] = inner * left_water
    gate[4] = inner * right_water

    def make_source(i, _):
        here = gate[0, pl.ds(i, 1), :]
        for level in range(levels):
            src[level, i] = fa[level, i] * here
        return 0

    lax.fori_loop(0, rows, make_source, 0)

    sub = lax.broadcasted_iota(jnp.int32, (recv, LANES), 0)

    def per_receptor(read):
        value = jnp.zeros((recv, LANES), jnp.float32)
        for r in range(recv):
            value = jnp.where(sub == r, read(r), value)
        return jnp.concatenate([value] * (width // LANES), 1)

    keep = per_receptor(lambda r: 1.0 - decay_ref[r])

    own_copy.wait()
    for copy in spread:
        copy.wait()

    def make_weights(hour):
        slot = plan_ref[hour]

        def tile(t, _):
            at = pl.ds(pl.multiple_of(t * SUBROWS, SUBROWS), SUBROWS)
            for level in range(levels):
                along = cur_buf[slot, 0, level, at, :].astype(jnp.float32)
                across = cur_buf[slot, 1, level, at, :].astype(jnp.float32)
                up = (jnp.maximum(-along, 0.0) + diffusion_number) * gate[1, at, :]
                down = (jnp.maximum(along, 0.0) + diffusion_number) * gate[2, at, :]
                left = (jnp.maximum(-across, 0.0) + diffusion_number) * gate[3, at, :]
                right = (jnp.maximum(across, 0.0) + diffusion_number) * gate[4, at, :]
                weight[0, level, at, :] = gate[0, at, :] - ((up + down) + (left + right))
                weight[1, level, at, :] = up
                weight[2, level, at, :] = down
                weight[3, level, at, :] = left
                weight[4, level, at, :] = right
            return 0

        lax.fori_loop(0, rows // SUBROWS, tile, 0)

    def do_row(fin, fout, i, upper, lower, obs):
        at = pl.ds(i, 1)

        def moved_at(level):
            center = fin[level, i]
            out = center * weight[0, level, at, :]
            out = out + upper(level) * weight[1, level, at, :]
            out = out + lower(level) * weight[2, level, at, :]
            out = out + pltpu.roll(center, 1, 1) * weight[3, level, at, :]
            return out + pltpu.roll(center, width - 1, 1) * weight[4, level, at, :]

        moved = moved_at(0)
        flux = None
        for level in range(levels):
            mixed = moved
            if flux is not None:
                mixed = mixed - flux
            if level < levels - 1:
                following = moved_at(level + 1)
                flux = mix_ref[level, at, :] * (following - moved)
                mixed = mixed + flux
                moved = following
            fout[level, i] = keep * mixed + obs * src[level, i]

    for step in range(HOURS):
        hour = HOURS - 1 - step
        fin, fout = (fa, fb) if step % 2 == 0 else (fb, fa)
        make_weights(hour)
        obs = per_receptor(lambda r: obs_ref[hour, r])
        finish(pair)
        do_row(
            fin, fout, 0,
            lambda level: halo[step, 0, level], lambda level: fin[level, 1], obs,
        )
        do_row(
            fin, fout, rows - 1,
            lambda level: fin[level, rows - 2], lambda level: halo[step, 1, level], obs,
        )
        if step < HOURS - 1:
            pair = halo_copies(step + 1, fout)
            start(pair)

        def interior(i, _):
            do_row(
                fin, fout, i,
                lambda level: fin[level, i - 1], lambda level: fin[level, i + 1], obs,
            )
            return 0

        lax.fori_loop(1, rows - 1, interior, 0)

    done = pltpu.make_async_copy(fout, out_hbm, out_sem)
    done.start()
    done.wait()


def run_steps(batches, strips, plan, decay, obs_weight, water, mixing, adjoint_end, currents):
    recv, levels, rows, width = adjoint_end.shape
    field = (levels, rows, recv, width)
    slots = currents.shape[0]
    vmem = pl.BlockSpec(memory_space=pltpu.VMEM)
    smem = pl.BlockSpec(memory_space=pltpu.SMEM)
    hbm = pl.BlockSpec(memory_space=pl.ANY)
    dma = pltpu.SemaphoreType.DMA
    return pl.pallas_call(
        functools.partial(steps_kernel, batches, strips),
        out_shape=jax.ShapeDtypeStruct(field, jnp.float32),
        in_specs=[smem, smem, smem, vmem, vmem, hbm, hbm],
        out_specs=hbm,
        scratch_shapes=[
            pltpu.VMEM((batches * slots,) + currents.shape[1:], currents.dtype),
            pltpu.VMEM(adjoint_end.shape, jnp.float32),
            pltpu.VMEM(field, jnp.float32),
            pltpu.VMEM(field, jnp.float32),
            pltpu.VMEM(field, jnp.float32),
            pltpu.VMEM((HOURS, 2, levels, recv, width), jnp.float32),
            pltpu.VMEM((2, 8, width), jnp.int32),
            pltpu.VMEM((5, rows, width), jnp.float32),
            pltpu.VMEM((5, levels, rows, width), jnp.float32),
            dma((batches - 1,)),
            dma((batches - 1,)),
            dma,
            dma((HOURS, 2)),
            dma((HOURS, 2)),
            dma((2,)),
            dma((2,)),
            dma((recv,)),
            dma,
        ],
        compiler_params=pltpu.CompilerParams(
            collective_id=0, has_side_effects=True, vmem_limit_bytes=VMEM_LIMIT
        ),
        name="transport_steps",
    )(plan, decay, obs_weight, water, mixing, adjoint_end, currents)


def sample_kernel(cells_ref, field_hbm, out_hbm, samples_ref, field, native, in_sem, out_sem):
    levels, rows, recv, width = field.shape
    blocks, block_cells = cells_ref.shape
    tiles = width // LANES
    load = pltpu.make_async_copy(field_hbm, field, in_sem)
    load.start()
    load.wait()

    def arrange(t, _):
        for level in range(levels):
            block = field[level, pl.ds(t * 8, 8)]
            native[:, level, pl.ds(pl.multiple_of(t * 8, 8), 8), :] = jnp.swapaxes(block, 0, 1)
        return 0

    lax.fori_loop(0, rows // 8, arrange, 0)
    stores = [
        pltpu.make_async_copy(native.at[r], out_hbm.at[r], out_sem.at[r]) for r in range(recv)
    ]
    for store in stores:
        store.start()

    group = 2 if blocks % 2 == 0 else 1

    def gather(g, _):
        lane, tile = [], []
        for k in range(group):
            cell = jnp.broadcast_to(cells_ref[pl.ds(g * group + k, 1), :], (recv, block_cells))
            lane.append(lax.rem(cell, LANES))
            tile.append(lax.div(cell, LANES))

        def row(i, totals):
            totals = list(totals)
            for c in range(tiles):
                hit = [tile[k] == i * tiles + c for k in range(group)]
                for level in range(levels):
                    values = field[level, i, :, c * LANES : (c + 1) * LANES]
                    for k in range(group):
                        picked = jnp.take_along_axis(
                            values, lane[k], axis=1, mode="promise_in_bounds"
                        )
                        at = k * levels + level
                        totals[at] = jnp.where(hit[k], picked, totals[at])
            return tuple(totals)

        zero = jnp.zeros((recv, block_cells), jnp.float32)
        totals = lax.fori_loop(0, rows, row, (zero,) * (group * levels))
        for k in range(group):
            for level in range(levels):
                samples_ref[
                    g * group + k, :, level * block_cells : (level + 1) * block_cells
                ] = totals[k * levels + level]
        return 0

    lax.fori_loop(0, blocks // group, gather, 0)
    for store in stores:
        store.wait()


def run_samples(cells, field):
    levels, rows, recv, width = field.shape
    blocks, block_cells = cells.shape
    vmem = pl.BlockSpec(memory_space=pltpu.VMEM)
    hbm = pl.BlockSpec(memory_space=pl.ANY)
    return pl.pallas_call(
        sample_kernel,
        out_shape=(
            jax.ShapeDtypeStruct((recv, levels, rows, width), jnp.float32),
            jax.ShapeDtypeStruct((blocks, recv, levels * block_cells), jnp.float32),
        ),
        in_specs=[vmem, hbm],
        out_specs=(hbm, vmem),
        scratch_shapes=[
            pltpu.VMEM(field.shape, jnp.float32),
            pltpu.VMEM((recv, levels, rows, width), jnp.float32),
            pltpu.SemaphoreType.DMA,
            pltpu.SemaphoreType.DMA((recv,)),
        ],
        compiler_params=pltpu.CompilerParams(vmem_limit_bytes=VMEM_LIMIT),
        name="release_samples",
    )(cells, field)


def contract_kernel(samples_ref, profiles_ref, out_ref):
    batches, own, recv, depth = samples_ref.shape
    for b in range(own):
        left = samples_ref[:, b].reshape(batches * recv, depth)
        out_ref[b] = jnp.dot(
            left, profiles_ref[b], precision=lax.Precision.HIGHEST,
            preferred_element_type=jnp.float32,
        )


def run_contract(gathered, profiles):
    batches, strips, own, recv, depth = gathered.shape
    scenarios = profiles.shape[-1]
    return pl.pallas_call(
        contract_kernel,
        grid=(strips,),
        out_shape=jax.ShapeDtypeStruct((strips, own, batches * recv, scenarios), jnp.float32),
        in_specs=[
            pl.BlockSpec((batches, None, own, recv, depth), lambda s: (0, s, 0, 0, 0)),
            pl.BlockSpec((None, own, depth, scenarios), lambda s: (s, 0, 0, 0)),
        ],
        out_specs=pl.BlockSpec((None, own, batches * recv, scenarios), lambda s: (s, 0, 0, 0)),
        compiler_params=pltpu.CompilerParams(vmem_limit_bytes=VMEM_LIMIT),
        name="scenario_response",
    )(gathered, profiles)


def on_device(
    adjoint_end, currents, plan, water_mask, mixing, decay, obs_weight, release_cells, profiles
):
    batches = lax.axis_size("rcpt")
    strips = lax.axis_size("space")
    stepped = run_steps(
        batches, strips, plan, decay, obs_weight, water_mask, mixing, adjoint_end, currents
    )
    field, samples = run_samples(release_cells[0], stepped)
    gathered = lax.all_to_all(samples, ("rcpt", "space"), split_axis=0, concat_axis=0, tiled=True)
    own = samples.shape[0] // (batches * strips)
    gathered = gathered.reshape((batches, strips, own) + samples.shape[1:])
    return (field, run_contract(gathered, profiles))


def solution(mesh):
    placed = (
        P("rcpt", None, "space", None),
        P("rcpt", None, None, "space", None),
        P(),
        P("space", None),
        P(None, "space", None),
        P("rcpt"),
        P(None, "rcpt"),
        P("space", None, None),
        P(None, ("rcpt", "space"), None, None),
    )
    return jax.shard_map(
        on_device,
        mesh=mesh,
        in_specs=placed,
        out_specs=(P("rcpt", None, "space", None), P(None, ("rcpt", "space"), None, None)),
        check_vma=False,
    )
```

time: 513 us -> 154 us (0.30); the launches traced: 507 us -> 154 us
  local copies, waits for them, and re-layouts: 313 us -> 4.93 us
  Pallas kernels: 0 us -> 127 us
  waiting for transfers between devices: 71.4 us -> 0 us
  other arithmetic: 71.1 us -> 0 us
  starting transfers between devices: 32.6 us -> 0 us
  blocking collectives: 0 us -> 21.2 us
  between operations: 17.5 us -> 0.68 us
    gather x2 -> x0, local copies, waits for them, and re-layouts: 243 us -> none  [on_device(): picked = jnp.take(flat, positions.reshape(-1), axis=1)]
    pallas_call x0 -> x3, Pallas kernels: none -> 127 us  [the longest x1 73.7 us: run_samples(): pl.pallas_call(sample_kernel, out_shape=(jax.ShapeDtypeStruct((recv, leve...]
    psum x1 -> x0, waiting for transfers between devices: 61.7 us -> none  [broadcast(): return lax.psum(kept, axis)]
    mul x11 -> x0, other arithmetic: 42.5 us -> none  [the longest x4 31.1 us: transport(): moved = moved * inner]
    add x3 -> x0, local copies, waits for them, and re-layouts: 30.5 us -> none  [the longest x1 30.4 us: on_device(): field = keep * mixed + obs_weight[hour_index][:, None, None, None] * source]
    ppermute x10 -> x0, starting transfers between devices: 27.3 us -> none  [the longest x5 20.7 us: with_halo(): lax.ppermute(lax.slice_in_dim(block, block.shape[dim] - width, None, axis...]
    add x5 -> x0, other arithmetic: 25 us -> none  [the longest x4 24.9 us: on_device(): field = keep * mixed + obs_weight[hour_index][:, None, None, None] * source]
    slice x12 -> x0, local copies, waits for them, and re-layouts: 24.7 us -> none  [the longest x5 23 us: next_column(): return jnp.concatenate([values[..., 1:], edge], -1)]
  transfers between devices with their start and end apart: 12 -> 0, of which waited for: 2 -> 0; matrix products, arithmetic and copies ran while one was open for 7% -> 0% of each run, Pallas kernels for 0% -> 0%
where the time goes in v1:
time: 154 us
  Pallas kernels  127 us (82%)
  blocking collectives  21.2 us (14%)
  local copies, waits for them, and re-layouts  4.93 us (3%)
    pallas_call x1, Pallas kernels, run_samples(): pl.pallas_call(sample_kernel, out_shape=(jax.ShapeDtypeStruct((recv, leve...  73.7 us
    pallas_call x1, Pallas kernels, run_steps(): pl.pallas_call(functools.partial(steps_kernel, batches, strips), out_shap...  49.8 us
    all_to_all x1, blocking collectives, on_device(): lax.all_to_all(samples, ('rcpt', 'space'), split_axis=0, concat_axis=0, t...  21.2 us
    unnamed x16, local copies, waits for them, and re-layouts  4.93 us
    pallas_call x1, Pallas kernels, run_contract(): pl.pallas_call(contract_kernel, grid=(strips,), out_shape=jax.ShapeDtypeS...  3.7 us

profile of v1, /device:TPU:0, one launch (start us, length us, event | category | flops | bytes accessed | tf_op | source)
XLA Modules:
  0.0 154.1 jit_solution(16333953777753191210)
XLA Ops:
  0.6 0.0 copy-start.1
  0.6 1.0 copy-done.1
  1.7 0.0 copy-start.2
  1.7 1.0 copy-done.2
  2.7 0.0 copy-start.3
  2.7 0.9 copy-done.3
  3.6 0.0 copy-start.5
  3.6 0.7 copy-done.5
  4.3 0.0 copy-start.6
  4.3 0.7 copy-done.6
  4.9 0.0 copy-start.7
  4.9 0.7 copy-done.7
  5.6 0.0 copy-start.4
  5.6 49.8 %transport_steps.1.field_hbm = f32[4,32,8,1024]{3,2,1,0:T(8,128)S(1)} custom-call(s32[4]{0:T(128)S(1)} %copy-done.6, f32[8]{0:T(128)S(1)} %copy-done.7, f32[4,8]{1,0:T(4,128)S(1)} %copy-done.5, s32[32,1024]{1,0:T(8,128)S(1)} %copy-done.3, f32[3,32,1024]{2,1,0:T(8,128)S(1)} %copy-done.2, f32[8,4,32,1024]{3,2,1,0:T(8,128)} %adj_hbm.1, ...), custom_call_target="tpu_custom_call" | custom-call | tf_op jit(solution)/shard_map/transport_steps/pallas_call | solution.py:270
  55.4 0.0 copy-start
  55.4 0.0 copy-done.4
  55.4 73.7 %release_samples.1 = (f32[8,4,32,1024]{3,2,1,0:T(8,128)}, f32[32,8,512]{2,1,0:T(8,128)S(1)}) custom-call(s32[32,128]{1,0:T(8,128)S(1)} %bitcast.3, f32[4,32,8,1024]{3,2,1,0:T(8,128)S(1)} %transport_steps.1.field_hbm), custom_call_target="tpu_custom_call" | custom-call | tf_op jit(solution)/shard_map/release_samples/pallas_call | solution.py:365
  129.2 21.2 %all_to_all.5 = f32[32,8,512]{2,1,0:T(8,128)S(1)} all-to-all(f32[32,8,512]{2,1,0:T(8,128)S(1)} %get-tuple-element.5), channel_id=1, replica_groups=mesh['rcpt'=4,'space'=8] {'rcpt','space'}, dimensions={0} | all-to-all | bytes 1048576 | tf_op jit(solution)/shard_map/all_to_all | solution.py:420
  150.4 0.0 copy-done
  150.4 3.7 %scenario_response.1 = f32[8,1,32,128]{3,2,1,0:T(8,128)} custom-call(f32[4,8,1,8,512]{4,3,2,1,0:T(8,128)S(1)} %bitcast.2, f32[8,1,512,128]{3,2,1,0:T(8,128)S(1)} %copy-done), custom_call_target="tpu_custom_call" | custom-call | tf_op jit(solution)/shard_map/scenario_response/pallas_call | solution.py:397
Async XLA Ops:
  0.6 1.0 copy-start.1
  1.7 1.0 copy-start.2
  2.7 0.9 copy-start.3
  3.6 0.7 copy-start.5
  4.3 0.7 copy-start.6
  4.9 0.7 copy-start.7
  5.6 49.9 %copy-start.4 = (s32[1,32,128]{2,1,0:T(8,128)S(1)}, s32[1,32,128]{2,1,0:T(8,128)}, u32[]{:S(2)}) copy-start(s32[1,32,128]{2,1,0:T(8,128)} %param.16) | copy-start | bytes 49156
  55.4 95.0 %copy-start = (f32[8,1,512,128]{3,2,1,0:T(8,128)S(1)}, f32[8,1,512,128]{3,2,1,0:T(8,128)}, u32[]{:S(2)}) copy-start(f32[8,1,512,128]{3,2,1,0:T(8,128)} %profiles_ref.1) | copy-start | bytes 6291460

commit v2 on v1

--- a/solution.py
+++ b/solution.py
@@ -18,10 +18,11 @@
 
 def steps_kernel(
     batches, strips,
-    plan_ref, decay_ref, obs_ref, water_ref, mix_ref, adj_hbm, cur_hbm,
+    plan_hbm, decay_hbm, obs_hbm, water_hbm, mix_hbm, adj_hbm, cur_hbm,
     out_hbm,
-    cur_buf, raw, fa, fb, src, halo, water_halo, gate, weight,
-    cur_send, cur_recv, cur_own, halo_send, halo_recv, wat_send, wat_recv, in_sem, out_sem,
+    plan_ref, decay_ref, obs_ref, water_ref, mix_ref,
+    cur_parts, raw, fa, fb, src, halo, water_halo, gate, weight,
+    cur_send, cur_recv, cur_own, halo_send, halo_recv, wat_send, wat_recv, in_sem, arg_sem, out_sem,
 ):
     recv, levels, rows, width = adj_hbm.shape
     slots = cur_hbm.shape[0]
@@ -49,31 +50,94 @@
     ]
     for load in loads:
         load.start()
-    own_slots = cur_buf.at[pl.ds(me * slots, slots)]
-    own_copy = pltpu.make_async_copy(cur_hbm, own_slots, cur_own)
-    own_copy.start()
+    pairs = (
+        (water_hbm, water_ref), (mix_hbm, mix_ref), (plan_hbm, plan_ref),
+        (decay_hbm, decay_ref), (obs_hbm, obs_ref),
+    )
+    args = [
+        pltpu.make_async_copy(there, here, arg_sem.at[k]) for k, (there, here) in enumerate(pairs)
+    ]
+    for arg in args:
+        arg.start()
+    parts = len(cur_parts)
+    part_rows = rows // parts
+
+    def slots_of(owner, part, component=None):
+        at = pl.ds(owner * slots, slots)
+        return cur_parts[part].at[at] if component is None else cur_parts[part].at[at, component]
+
+    def stored(part):
+        return cur_hbm.at[:, :, :, pl.ds(part * part_rows, part_rows)]
+
+    own_copies = [
+        pltpu.make_async_copy(stored(part), slots_of(me, part), cur_own.at[part])
+        for part in range(parts)
+    ]
+    for copy in own_copies:
+        copy.start()
 
     peers = batches - 1 + has_up.astype(jnp.int32) + has_down.astype(jnp.int32)
     pl.semaphore_wait(barrier, peers)
 
-    spread = []
-    for d in range(1, batches):
-        copy = pltpu.make_async_remote_copy(
-            src_ref=cur_hbm, dst_ref=own_slots,
-            send_sem=cur_send.at[d - 1], recv_sem=cur_recv.at[d - 1],
-            device_id={"rcpt": lax.rem(me + d, batches)}, device_id_type=MESH,
-        )
-        copy.start()
-        spread.append(copy)
+    def send(part, k, source, target, peer):
+        return pltpu.make_async_remote_copy(
+            src_ref=source, dst_ref=target,
+            send_sem=cur_send.at[part, k], recv_sem=cur_recv.at[part, k],
+            device_id={"rcpt": peer}, device_id_type=MESH,
+        )
+
+    square = batches == 4
+    if square:
+        side = me + 1 - 2 * lax.rem(me, 2)
+        other = lax.rem(me + 2, batches)
+        partners = (side, other)
+    else:
+        partners = tuple(lax.rem(me + d, batches) for d in range(1, batches))
+    spread = [
+        [
+            send(
+                part, k, stored(part), slots_of(me, part), peer,
+            )
+            for k, peer in enumerate(partners)
+        ]
+        for part in range(parts)
+    ]
+    passed = []
+    if square:
+        passed = [
+            [
+                send(part, 2, slots_of(other, part, 0), slots_of(other, part, 0), side),
+                send(part, 3, slots_of(side, part, 1), slots_of(side, part, 1), other),
+            ]
+            for part in range(parts)
+        ]
+    for copies in spread:
+        for copy in copies:
+            copy.start()
+
+    def pass_on(part):
+        if square:
+            spread[part][1].wait_recv()
+            passed[part][0].start()
+            spread[part][0].wait_recv()
+            passed[part][1].start()
+
+    def arrived(part):
+        if square:
+            for copy in passed[part]:
+                copy.wait_recv()
+        else:
+            for copy in spread[part]:
+                copy.wait_recv()
 
     def water_copies():
         up = pltpu.make_async_remote_copy(
-            src_ref=water_ref.at[pl.ds(0, 8)], dst_ref=water_halo.at[1],
+            src_ref=water_hbm.at[pl.ds(0, 8)], dst_ref=water_halo.at[1],
             send_sem=wat_send.at[0], recv_sem=wat_recv.at[0],
             device_id={"space": strip - 1}, device_id_type=MESH,
         )
         down = pltpu.make_async_remote_copy(
-            src_ref=water_ref.at[pl.ds(rows - 8, 8)], dst_ref=water_halo.at[0],
+            src_ref=water_hbm.at[pl.ds(rows - 8, 8)], dst_ref=water_halo.at[0],
             send_sem=wat_send.at[1], recv_sem=wat_recv.at[1],
             device_id={"space": strip + 1}, device_id_type=MESH,
         )
@@ -144,6 +208,8 @@
         for step in range(HOURS):
             halo[step, 1] = jnp.zeros_like(halo[step, 1])
 
+    for arg in args:
+        arg.wait()
     finish(water_pair)
     inner = water_ref[...].astype(jnp.float32)
     above = water_halo[0, 7:8, :].astype(jnp.float32)
@@ -178,41 +244,38 @@
 
     keep = per_receptor(lambda r: 1.0 - decay_ref[r])
 
-    own_copy.wait()
-    for copy in spread:
-        copy.wait()
-
-    def make_weights(hour):
-        slot = plan_ref[hour]
+    def make_weights(part):
+        buffer = cur_parts[part]
 
         def tile(t, _):
-            at = pl.ds(pl.multiple_of(t * SUBROWS, SUBROWS), SUBROWS)
-            for level in range(levels):
-                along = cur_buf[slot, 0, level, at, :].astype(jnp.float32)
-                across = cur_buf[slot, 1, level, at, :].astype(jnp.float32)
-                up = (jnp.maximum(-along, 0.0) + diffusion_number) * gate[1, at, :]
-                down = (jnp.maximum(along, 0.0) + diffusion_number) * gate[2, at, :]
-                left = (jnp.maximum(-across, 0.0) + diffusion_number) * gate[3, at, :]
-                right = (jnp.maximum(across, 0.0) + diffusion_number) * gate[4, at, :]
-                weight[0, level, at, :] = gate[0, at, :] - ((up + down) + (left + right))
-                weight[1, level, at, :] = up
-                weight[2, level, at, :] = down
-                weight[3, level, at, :] = left
-                weight[4, level, at, :] = right
+            held = pl.ds(pl.multiple_of(t * SUBROWS, SUBROWS), SUBROWS)
+            at = pl.ds(pl.multiple_of(part * part_rows + t * SUBROWS, SUBROWS), SUBROWS)
+            for hour in range(HOURS):
+                slot = plan_ref[hour]
+                for level in range(levels):
+                    along = buffer[slot, 0, level, held, :].astype(jnp.float32)
+                    across = buffer[slot, 1, level, held, :].astype(jnp.float32)
+                    up = (jnp.maximum(-along, 0.0) + diffusion_number) * gate[1, at, :]
+                    down = (jnp.maximum(along, 0.0) + diffusion_number) * gate[2, at, :]
+                    left = (jnp.maximum(-across, 0.0) + diffusion_number) * gate[3, at, :]
+                    right = (jnp.maximum(across, 0.0) + diffusion_number) * gate[4, at, :]
+                    middle = gate[0, at, :] - ((up + down) + (left + right))
+                    for k, value in enumerate((middle, up, down, left, right)):
+                        weight[hour, k, level, at, :] = value
             return 0
 
-        lax.fori_loop(0, rows // SUBROWS, tile, 0)
-
-    def do_row(fin, fout, i, upper, lower, obs):
+        lax.fori_loop(0, part_rows // SUBROWS, tile, 0)
+
+    def do_row(hour, fin, fout, i, upper, lower, obs):
         at = pl.ds(i, 1)
 
         def moved_at(level):
             center = fin[level, i]
-            out = center * weight[0, level, at, :]
-            out = out + upper(level) * weight[1, level, at, :]
-            out = out + lower(level) * weight[2, level, at, :]
-            out = out + pltpu.roll(center, 1, 1) * weight[3, level, at, :]
-            return out + pltpu.roll(center, width - 1, 1) * weight[4, level, at, :]
+            out = center * weight[hour, 0, level, at, :]
+            out = out + upper(level) * weight[hour, 1, level, at, :]
+            out = out + lower(level) * weight[hour, 2, level, at, :]
+            out = out + pltpu.roll(center, 1, 1) * weight[hour, 3, level, at, :]
+            return out + pltpu.roll(center, width - 1, 1) * weight[hour, 4, level, at, :]
 
         moved = moved_at(0)
         flux = None
@@ -227,33 +290,71 @@
                 moved = following
             fout[level, i] = keep * mixed + obs * src[level, i]
 
-    for step in range(HOURS):
+    seen = [per_receptor(lambda r, h=h: obs_ref[h, r]) for h in range(HOURS)]
+
+    def buffers(step):
+        return (fa, fb) if step % 2 == 0 else (fb, fa)
+
+    def span(step, low, high):
         hour = HOURS - 1 - step
-        fin, fout = (fa, fb) if step % 2 == 0 else (fb, fa)
-        make_weights(hour)
-        obs = per_receptor(lambda r: obs_ref[hour, r])
-        finish(pair)
-        do_row(
-            fin, fout, 0,
-            lambda level: halo[step, 0, level], lambda level: fin[level, 1], obs,
-        )
-        do_row(
-            fin, fout, rows - 1,
-            lambda level: fin[level, rows - 2], lambda level: halo[step, 1, level], obs,
-        )
-        if step < HOURS - 1:
-            pair = halo_copies(step + 1, fout)
-            start(pair)
-
-        def interior(i, _):
+        fin, fout = buffers(step)
+
+        def body(i, _):
             do_row(
-                fin, fout, i,
-                lambda level: fin[level, i - 1], lambda level: fin[level, i + 1], obs,
+                hour, fin, fout, i,
+                lambda level: fin[level, i - 1], lambda level: fin[level, i + 1], seen[hour],
             )
             return 0
 
-        lax.fori_loop(1, rows - 1, interior, 0)
-
+        if low < high:
+            lax.fori_loop(low, high, body, 0)
+
+    def first_row(step):
+        hour = HOURS - 1 - step
+        fin, fout = buffers(step)
+        do_row(
+            hour, fin, fout, 0,
+            lambda level: halo[step, 0, level], lambda level: fin[level, 1], seen[hour],
+        )
+
+    def last_row(step):
+        hour = HOURS - 1 - step
+        fin, fout = buffers(step)
+        do_row(
+            hour, fin, fout, rows - 1,
+            lambda level: fin[level, rows - 2], lambda level: halo[step, 1, level], seen[hour],
+        )
+
+    for copy in own_copies:
+        copy.wait()
+    pass_on(0)
+    for part in range(parts):
+        arrived(part)
+        if part < parts - 1:
+            make_weights(part)
+            for step in range(HOURS):
+                span(step, step + 1, part_rows - 1 - step)
+                if step == 0:
+                    pass_on(part + 1)
+    make_weights(parts - 1)
+    early = parts > 1
+    for step in range(HOURS):
+        finish(pair)
+        first_row(step)
+        last_row(step)
+        if step < HOURS - 1:
+            pair = halo_copies(step + 1, buffers(step)[1])
+            start(pair)
+        if early:
+            span(step, 1, step + 1)
+            span(step, max(part_rows - 1 - step, step + 1), rows - 1)
+        else:
+            span(step, 1, rows - 1)
+    for copies in spread + passed:
+        for copy in copies:
+            copy.wait_send()
+
+    fout = buffers(HOURS - 1)[1]
     done = pltpu.make_async_copy(fout, out_hbm, out_sem)
     done.start()
     done.wait()
@@ -263,17 +364,26 @@
     recv, levels, rows, width = adjoint_end.shape
     field = (levels, rows, recv, width)
     slots = currents.shape[0]
-    vmem = pl.BlockSpec(memory_space=pltpu.VMEM)
-    smem = pl.BlockSpec(memory_space=pltpu.SMEM)
+    parts = 2 if rows % (2 * SUBROWS) == 0 else 1
     hbm = pl.BlockSpec(memory_space=pl.ANY)
     dma = pltpu.SemaphoreType.DMA
     return pl.pallas_call(
         functools.partial(steps_kernel, batches, strips),
         out_shape=jax.ShapeDtypeStruct(field, jnp.float32),
-        in_specs=[smem, smem, smem, vmem, vmem, hbm, hbm],
+        in_specs=[hbm] * 7,
         out_specs=hbm,
         scratch_shapes=[
-            pltpu.VMEM((batches * slots,) + currents.shape[1:], currents.dtype),
+            pltpu.SMEM(plan.shape, jnp.int32),
+            pltpu.SMEM(decay.shape, jnp.float32),
+            pltpu.SMEM(obs_weight.shape, jnp.float32),
+            pltpu.VMEM(water.shape, jnp.int32),
+            pltpu.VMEM(mixing.shape, jnp.float32),
+            [
+                pltpu.VMEM(
+                    (batches * slots, 2, levels, rows // parts, width), currents.dtype
+                )
+            ]
+            * parts,
             pltpu.VMEM(adjoint_end.shape, jnp.float32),
             pltpu.VMEM(field, jnp.float32),
             pltpu.VMEM(field, jnp.float32),
@@ -281,15 +391,16 @@
             pltpu.VMEM((HOURS, 2, levels, recv, width), jnp.float32),
             pltpu.VMEM((2, 8, width), jnp.int32),
             pltpu.VMEM((5, rows, width), jnp.float32),
-            pltpu.VMEM((5, levels, rows, width), jnp.float32),
-            dma((batches - 1,)),
-            dma((batches - 1,)),
-            dma,
+            pltpu.VMEM((HOURS, 5, levels, rows, width), jnp.float32),
+            dma((parts, max(batches - 1, 4))),
+            dma((parts, max(batches - 1, 4))),
+            dma((parts,)),
             dma((HOURS, 2)),
             dma((HOURS, 2)),
             dma((2,)),
             dma((2,)),
             dma((recv,)),
+            dma((5,)),
             dma,
         ],
         compiler_params=pltpu.CompilerParams(
@@ -299,12 +410,25 @@
     )(plan, decay, obs_weight, water, mixing, adjoint_end, currents)
 
 
-def sample_kernel(cells_ref, field_hbm, out_hbm, samples_ref, field, native, in_sem, out_sem):
+def sample_kernel(
+    cells_hbm, field_hbm, out_hbm, samples_ref,
+    cells_ref, field, native, by_cell, picked, places, places_ref,
+    cell_sem, place_sem, in_sem, out_sem,
+):
     levels, rows, recv, width = field.shape
     blocks, block_cells = cells_ref.shape
     tiles = width // LANES
+    packed = LANES // (levels * recv)
     load = pltpu.make_async_copy(field_hbm, field, in_sem)
     load.start()
+    cell_load = pltpu.make_async_copy(cells_hbm, cells_ref, cell_sem)
+    cell_load.start()
+    cell_load.wait()
+    cells = cells_ref[...]
+    tile = lax.div(cells, LANES)
+    places[...] = lax.div(tile, packed) * LANES + lax.rem(cells, LANES)
+    place_copy = pltpu.make_async_copy(places, places_ref, place_sem)
+    place_copy.start()
     load.wait()
 
     def arrange(t, _):
@@ -320,39 +444,40 @@
     for store in stores:
         store.start()
 
-    group = 2 if blocks % 2 == 0 else 1
-
-    def gather(g, _):
-        lane, tile = [], []
-        for k in range(group):
-            cell = jnp.broadcast_to(cells_ref[pl.ds(g * group + k, 1), :], (recv, block_cells))
-            lane.append(lax.rem(cell, LANES))
-            tile.append(lax.div(cell, LANES))
-
-        def row(i, totals):
-            totals = list(totals)
-            for c in range(tiles):
-                hit = [tile[k] == i * tiles + c for k in range(group)]
-                for level in range(levels):
-                    values = field[level, i, :, c * LANES : (c + 1) * LANES]
-                    for k in range(group):
-                        picked = jnp.take_along_axis(
-                            values, lane[k], axis=1, mode="promise_in_bounds"
-                        )
-                        at = k * levels + level
-                        totals[at] = jnp.where(hit[k], picked, totals[at])
-            return tuple(totals)
-
-        zero = jnp.zeros((recv, block_cells), jnp.float32)
-        totals = lax.fori_loop(0, rows, row, (zero,) * (group * levels))
-        for k in range(group):
-            for level in range(levels):
-                samples_ref[
-                    g * group + k, :, level * block_cells : (level + 1) * block_cells
-                ] = totals[k * levels + level]
+    groups = tiles // packed
+
+    def turn(i, _):
+        for g in range(groups):
+            stack = jnp.concatenate(
+                [
+                    field[level, i, :, (g * packed + q) * LANES : (g * packed + q + 1) * LANES]
+                    for q in range(packed)
+                    for level in range(levels)
+                ],
+                0,
+            )
+            at = pl.multiple_of((i * groups + g) * LANES, LANES)
+            by_cell[pl.ds(at, LANES), :] = stack.T
         return 0
 
-    lax.fori_loop(0, blocks // group, gather, 0)
+    lax.fori_loop(0, rows, turn, 0)
+    place_copy.wait()
+
+    def pick(b, _):
+        for c in range(block_cells):
+            picked[pl.ds(c, 1), :] = by_cell[pl.ds(places_ref[b, c], 1), :]
+        turned = picked[...].T
+        cell = jnp.broadcast_to(cells_ref[pl.ds(b, 1), :], (recv, block_cells))
+        which = lax.rem(lax.div(cell, LANES), packed)
+        for level in range(levels):
+            value = turned[level * recv : (level + 1) * recv]
+            for q in range(1, packed):
+                at = (q * levels + level) * recv
+                value = jnp.where(which == q, turned[at : at + recv], value)
+            samples_ref[b, :, level * block_cells : (level + 1) * block_cells] = value
+        return 0
+
+    lax.fori_loop(0, blocks, pick, 0)
     for store in stores:
         store.wait()
 
@@ -360,6 +485,7 @@
 def run_samples(cells, field):
     levels, rows, recv, width = field.shape
     blocks, block_cells = cells.shape
+    packed = LANES // (levels * recv)
     vmem = pl.BlockSpec(memory_space=pltpu.VMEM)
     hbm = pl.BlockSpec(memory_space=pl.ANY)
     return pl.pallas_call(
@@ -368,11 +494,18 @@
             jax.ShapeDtypeStruct((recv, levels, rows, width), jnp.float32),
             jax.ShapeDtypeStruct((blocks, recv, levels * block_cells), jnp.float32),
         ),
-        in_specs=[vmem, hbm],
+        in_specs=[hbm, hbm],
         out_specs=(hbm, vmem),
         scratch_shapes=[
+            pltpu.VMEM(cells.shape, jnp.int32),
             pltpu.VMEM(field.shape, jnp.float32),
             pltpu.VMEM((recv, levels, rows, width), jnp.float32),
+            pltpu.VMEM((rows * width // packed, LANES), jnp.float32),
+            pltpu.VMEM((block_cells, LANES), jnp.float32),
+            pltpu.VMEM(cells.shape, jnp.int32),
+            pltpu.SMEM(cells.shape, jnp.int32),
+            pltpu.SemaphoreType.DMA,
+            pltpu.SemaphoreType.DMA,
             pltpu.SemaphoreType.DMA,
             pltpu.SemaphoreType.DMA((recv,)),
         ],

time: 154 us -> 83.7 us (0.54)
  Pallas kernels: 127 us -> 55.3 us
    pallas_call x1, Pallas kernels: 73.7 us -> 10.7 us  [run_samples(): pl.pallas_call(sample_kernel, out_shape=(jax.ShapeDtypeStruct((recv, leve...]
    pallas_call x1, Pallas kernels: 49.8 us -> 40.9 us  [run_steps(): pl.pallas_call(functools.partial(steps_kernel, batches, strips), out_shap...]
where the time goes in v2:
time: 83.7 us; the launch traced here: 83.4 us
  Pallas kernels  55.3 us (66%)
  blocking collectives  22.5 us (27%)
  local copies, waits for them, and re-layouts  4.93 us (6%)
    pallas_call x1, Pallas kernels, run_steps(): pl.pallas_call(functools.partial(steps_kernel, batches, strips), out_shap...  40.9 us
    all_to_all x1, blocking collectives, on_device(): lax.all_to_all(samples, ('rcpt', 'space'), split_axis=0, concat_axis=0, t...  22.5 us
    pallas_call x1, Pallas kernels, run_samples(): pl.pallas_call(sample_kernel, out_shape=(jax.ShapeDtypeStruct((recv, leve...  10.7 us
    unnamed x16, local copies, waits for them, and re-layouts  4.93 us
    pallas_call x1, Pallas kernels, run_contract(): pl.pallas_call(contract_kernel, grid=(strips,), out_shape=jax.ShapeDtypeS...  3.7 us

profile of v2, /device:TPU:0, one launch (start us, length us, event | category | flops | bytes accessed | tf_op | source)
XLA Modules:
  0.0 83.4 jit_solution(17657171589291325688)
XLA Ops:
  0.6 0.0 copy-start.1
  0.6 1.0 %copy-done.1 = bf16[1,2,4,32,1024]{4,3,2,1,0:T(8,128)(2,1)S(1)} copy-done((bf16[1,2,4,32,1024]{4,3,2,1,0:T(8,128)(2,1)S(1)}, bf16[1,2,4,32,1024]{4,3,2,1,0:T(8,128)(2,1)}, u32[]{:S(2)}) %copy-start.1) | copy-done | bytes 524312
  1.7 0.0 copy-start.2
  1.7 1.0 %copy-done.2 = f32[3,32,1024]{2,1,0:T(8,128)S(1)} copy-done((f32[3,32,1024]{2,1,0:T(8,128)S(1)}, f32[3,32,1024]{2,1,0:T(8,128)}, u32[]{:S(2)}) %copy-start.2) | copy-done | bytes 393240
  2.7 0.0 copy-start.3
  2.7 0.9 %copy-done.3 = s32[32,1024]{1,0:T(8,128)S(1)} copy-done((s32[32,1024]{1,0:T(8,128)S(1)}, s32[32,1024]{1,0:T(8,128)}, u32[]{:S(2)}) %copy-start.3) | copy-done | bytes 131096
  3.6 0.0 copy-start.5
  3.6 0.7 copy-done.5
  4.3 0.0 copy-start.6
  4.3 0.7 copy-done.6
  4.9 0.0 copy-start.7
  4.9 0.7 copy-done.7
  5.6 0.0 copy-start.4
  5.6 40.9 %transport_steps.1.field_hbm = f32[4,32,8,1024]{3,2,1,0:T(8,128)S(1)} custom-call(s32[4]{0:T(128)S(1)} %copy-done.6, f32[8]{0:T(128)S(1)} %copy-done.7, f32[4,8]{1,0:T(4,128)S(1)} %copy-done.5, s32[32,1024]{1,0:T(8,128)S(1)} %copy-done.3, f32[3,32,1024]{2,1,0:T(8,128)S(1)} %copy-done.2, f32[8,4,32,1024]{3,2,1,0:T(8,128)} %adj_hbm.1, ...), custom_call_target="tpu_custom_call" | custom-call | tf_op jit(solution)/shard_map/transport_steps/pallas_call | solution.py:370
  46.4 0.0 copy-start
  46.5 0.0 copy-done.4
  46.5 10.7 %release_samples.1 = (f32[8,4,32,1024]{3,2,1,0:T(8,128)}, f32[32,8,512]{2,1,0:T(8,128)S(1)}) custom-call(s32[32,128]{1,0:T(8,128)S(1)} %bitcast.3, f32[4,32,8,1024]{3,2,1,0:T(8,128)S(1)} %transport_steps.1.field_hbm), custom_call_target="tpu_custom_call" | custom-call | tf_op jit(solution)/shard_map/release_samples/pallas_call | solution.py:491
  57.2 22.5 %all_to_all.5 = f32[32,8,512]{2,1,0:T(8,128)S(1)} all-to-all(f32[32,8,512]{2,1,0:T(8,128)S(1)} %get-tuple-element.5), channel_id=1, replica_groups=mesh['rcpt'=4,'space'=8] {'rcpt','space'}, dimensions={0} | all-to-all | bytes 1048576 | tf_op jit(solution)/shard_map/all_to_all | solution.py:553
  79.7 0.0 copy-done
  79.7 3.7 %scenario_response.1 = f32[8,1,32,128]{3,2,1,0:T(8,128)} custom-call(f32[4,8,1,8,512]{4,3,2,1,0:T(8,128)S(1)} %bitcast.2, f32[8,1,512,128]{3,2,1,0:T(8,128)S(1)} %copy-done), custom_call_target="tpu_custom_call" | custom-call | tf_op jit(solution)/shard_map/scenario_response/pallas_call | solution.py:530
Async XLA Ops:
  0.6 1.0 %copy-start.1 = (bf16[1,2,4,32,1024]{4,3,2,1,0:T(8,128)(2,1)S(1)}, bf16[1,2,4,32,1024]{4,3,2,1,0:T(8,128)(2,1)}, u32[]{:S(2)}) copy-start(bf16[1,2,4,32,1024]{4,3,2,1,0:T(8,128)(2,1)} %cur_hbm.1) | copy-start | bytes 1572868
  1.7 1.0 %copy-start.2 = (f32[3,32,1024]{2,1,0:T(8,128)S(1)}, f32[3,32,1024]{2,1,0:T(8,128)}, u32[]{:S(2)}) copy-start(f32[3,32,1024]{2,1,0:T(8,128)} %mix_hbm.1) | copy-start | bytes 1179652
  2.7 0.9 %copy-start.3 = (s32[32,1024]{1,0:T(8,128)S(1)}, s32[32,1024]{1,0:T(8,128)}, u32[]{:S(2)}) copy-start(s32[32,1024]{1,0:T(8,128)} %water_hbm.1) | copy-start | bytes 393220
  3.6 0.7 copy-start.5
  4.3 0.7 copy-start.6
  4.9 0.7 copy-start.7
  5.6 40.9 %copy-start.4 = (s32[1,32,128]{2,1,0:T(8,128)S(1)}, s32[1,32,128]{2,1,0:T(8,128)}, u32[]{:S(2)}) copy-start(s32[1,32,128]{2,1,0:T(8,128)} %param.16) | copy-start | bytes 49156
  46.4 33.3 %copy-start = (f32[8,1,512,128]{3,2,1,0:T(8,128)S(1)}, f32[8,1,512,128]{3,2,1,0:T(8,128)}, u32[]{:S(2)}) copy-start(f32[8,1,512,128]{3,2,1,0:T(8,128)} %profiles_ref.1) | copy-start | bytes 6291460

commit v3 on v2

--- a/solution.py
+++ b/solution.py
@@ -11,7 +11,7 @@
 LANES = 128
 SUBROWS = 16
 MESH = pl.DeviceIdType.MESH
-VMEM_LIMIT = 48 * 1024 * 1024
+VMEM_LIMIT = 63 * 1024 * 1024
 
 diffusion_number = 0.08
 
@@ -345,19 +345,25 @@
         if step < HOURS - 1:
             pair = halo_copies(step + 1, buffers(step)[1])
             start(pair)
+        low = max(part_rows - 1 - step, step + 1) if early else 1
         if early:
             span(step, 1, step + 1)
-            span(step, max(part_rows - 1 - step, step + 1), rows - 1)
-        else:
-            span(step, 1, rows - 1)
+        if step < HOURS - 1:
+            span(step, low, rows - 1)
+    result = buffers(HOURS - 1)[1]
+    leaving = []
+    for t in range(rows // 8):
+        span(HOURS - 1, max(low, t * 8), min(rows - 1, t * 8 + 8))
+        piece = pl.ds(t * 8, 8)
+        leaving.append(
+            pltpu.make_async_copy(result.at[:, piece], out_hbm.at[:, piece], out_sem.at[t])
+        )
+        leaving[-1].start()
+    for copy in leaving:
+        copy.wait()
     for copies in spread + passed:
         for copy in copies:
             copy.wait_send()
-
-    fout = buffers(HOURS - 1)[1]
-    done = pltpu.make_async_copy(fout, out_hbm, out_sem)
-    done.start()
-    done.wait()
 
 
 def run_steps(batches, strips, plan, decay, obs_weight, water, mixing, adjoint_end, currents):
@@ -401,7 +407,7 @@
             dma((2,)),
             dma((recv,)),
             dma((5,)),
-            dma,
+            dma((rows // 8,)),
         ],
         compiler_params=pltpu.CompilerParams(
             collective_id=0, has_side_effects=True, vmem_limit_bytes=VMEM_LIMIT
@@ -410,41 +416,18 @@
     )(plan, decay, obs_weight, water, mixing, adjoint_end, currents)
 
 
-def sample_kernel(
-    cells_hbm, field_hbm, out_hbm, samples_ref,
-    cells_ref, field, native, by_cell, picked, places, places_ref,
-    cell_sem, place_sem, in_sem, out_sem,
-):
+def turn_kernel(field_hbm, out_hbm, by_cell_hbm, field, native, by_cell, in_sem, out_sem, cell_sem):
     levels, rows, recv, width = field.shape
-    blocks, block_cells = cells_ref.shape
     tiles = width // LANES
     packed = LANES // (levels * recv)
-    load = pltpu.make_async_copy(field_hbm, field, in_sem)
-    load.start()
-    cell_load = pltpu.make_async_copy(cells_hbm, cells_ref, cell_sem)
-    cell_load.start()
-    cell_load.wait()
-    cells = cells_ref[...]
-    tile = lax.div(cells, LANES)
-    places[...] = lax.div(tile, packed) * LANES + lax.rem(cells, LANES)
-    place_copy = pltpu.make_async_copy(places, places_ref, place_sem)
-    place_copy.start()
-    load.wait()
-
-    def arrange(t, _):
-        for level in range(levels):
-            block = field[level, pl.ds(t * 8, 8)]
-            native[:, level, pl.ds(pl.multiple_of(t * 8, 8), 8), :] = jnp.swapaxes(block, 0, 1)
-        return 0
-
-    lax.fori_loop(0, rows // 8, arrange, 0)
-    stores = [
-        pltpu.make_async_copy(native.at[r], out_hbm.at[r], out_sem.at[r]) for r in range(recv)
+    groups = tiles // packed
+    pieces = [pl.ds(t * 8, 8) for t in range(rows // 8)]
+    loads = [
+        pltpu.make_async_copy(field_hbm.at[:, piece], field.at[:, piece], in_sem.at[t])
+        for t, piece in enumerate(pieces)
     ]
-    for store in stores:
-        store.start()
-
-    groups = tiles // packed
+    for load in loads:
+        load.start()
 
     def turn(i, _):
         for g in range(groups):
@@ -460,85 +443,209 @@
             by_cell[pl.ds(at, LANES), :] = stack.T
         return 0
 
-    lax.fori_loop(0, rows, turn, 0)
-    place_copy.wait()
-
-    def pick(b, _):
-        for c in range(block_cells):
-            picked[pl.ds(c, 1), :] = by_cell[pl.ds(places_ref[b, c], 1), :]
-        turned = picked[...].T
-        cell = jnp.broadcast_to(cells_ref[pl.ds(b, 1), :], (recv, block_cells))
-        which = lax.rem(lax.div(cell, LANES), packed)
+    leaving = []
+    for t, piece in enumerate(pieces):
+        loads[t].wait()
         for level in range(levels):
-            value = turned[level * recv : (level + 1) * recv]
-            for q in range(1, packed):
-                at = (q * levels + level) * recv
-                value = jnp.where(which == q, turned[at : at + recv], value)
-            samples_ref[b, :, level * block_cells : (level + 1) * block_cells] = value
-        return 0
-
-    lax.fori_loop(0, blocks, pick, 0)
-    for store in stores:
-        store.wait()
-
-
-def run_samples(cells, field):
+            native[:, level, piece, :] = jnp.swapaxes(field[level, piece], 0, 1)
+        leaving.append(
+            pltpu.make_async_copy(
+                native.at[:, :, piece], out_hbm.at[:, :, piece], out_sem.at[t]
+            )
+        )
+        leaving[-1].start()
+        lax.fori_loop(t * 8, t * 8 + 8, turn, 0)
+        held = pl.ds(t * 8 * groups * LANES, 8 * groups * LANES)
+        leaving.append(
+            pltpu.make_async_copy(by_cell.at[held], by_cell_hbm.at[held], cell_sem.at[t])
+        )
+        leaving[-1].start()
+    for copy in leaving:
+        copy.wait()
+
+
+def run_turn(field):
     levels, rows, recv, width = field.shape
-    blocks, block_cells = cells.shape
     packed = LANES // (levels * recv)
-    vmem = pl.BlockSpec(memory_space=pltpu.VMEM)
+    by_cell = (rows * width // packed, LANES)
     hbm = pl.BlockSpec(memory_space=pl.ANY)
     return pl.pallas_call(
-        sample_kernel,
+        turn_kernel,
         out_shape=(
             jax.ShapeDtypeStruct((recv, levels, rows, width), jnp.float32),
-            jax.ShapeDtypeStruct((blocks, recv, levels * block_cells), jnp.float32),
+            jax.ShapeDtypeStruct(by_cell, jnp.float32),
         ),
-        in_specs=[hbm, hbm],
-        out_specs=(hbm, vmem),
+        in_specs=[hbm],
+        out_specs=(hbm, hbm),
         scratch_shapes=[
-            pltpu.VMEM(cells.shape, jnp.int32),
             pltpu.VMEM(field.shape, jnp.float32),
             pltpu.VMEM((recv, levels, rows, width), jnp.float32),
-            pltpu.VMEM((rows * width // packed, LANES), jnp.float32),
-            pltpu.VMEM((block_cells, LANES), jnp.float32),
+            pltpu.VMEM(by_cell, jnp.float32),
+            pltpu.SemaphoreType.DMA((rows // 8,)),
+            pltpu.SemaphoreType.DMA((rows // 8,)),
+            pltpu.SemaphoreType.DMA((rows // 8,)),
+        ],
+        compiler_params=pltpu.CompilerParams(vmem_limit_bytes=VMEM_LIMIT),
+        name="cell_major",
+    )(field)
+
+
+def response_kernel(
+    batches, strips, recv, levels,
+    cells_hbm, by_cell_hbm, profiles_hbm, out_ref,
+    by_cell, profiles_ref, cells_ref, places, places_ref, picked, sending, landed,
+    cell_sem, place_sem, load_sem, send_sem, recv_sem,
+):
+    blocks, block_cells = cells_ref.shape
+    own = blocks // (batches * strips)
+    packed = LANES // (levels * recv)
+    batch = lax.axis_index("rcpt")
+    strip = lax.axis_index("space")
+    cell_load = pltpu.make_async_copy(cells_hbm, cells_ref, cell_sem)
+    cell_load.start()
+    load = pltpu.make_async_copy(by_cell_hbm, by_cell, load_sem.at[0])
+    load.start()
+    profile_load = pltpu.make_async_copy(profiles_hbm, profiles_ref, load_sem.at[1])
+    profile_load.start()
+
+    barrier = pltpu.get_barrier_semaphore()
+
+    def peer(j, i):
+        return {"rcpt": lax.rem(batch + i, batches), "space": lax.rem(strip + j, strips)}
+
+    for i in range(1, batches):
+        pl.semaphore_signal(barrier, inc=1, device_id=peer(0, i), device_id_type=MESH)
+
+    def greet(j, _):
+        for i in range(batches):
+            pl.semaphore_signal(barrier, inc=1, device_id=peer(j, i), device_id_type=MESH)
+        return 0
+
+    lax.fori_loop(1, strips, greet, 0)
+
+    cell_load.wait()
+    cells = cells_ref[...]
+    places[...] = lax.div(lax.div(cells, LANES), packed) * LANES + lax.rem(cells, LANES)
+    place_copy = pltpu.make_async_copy(places, places_ref, place_sem)
+    place_copy.start()
+    place_copy.wait()
+    load.wait()
+
+    def pick(j, i, put):
+        target = peer(j, i)
+        first = (target["rcpt"] * strips + target["space"]) * own
+        for k in range(own):
+            b = first + k
+            for c in range(block_cells):
+                picked[pl.ds(c, 1), :] = by_cell[pl.ds(places_ref[b, c], 1), :]
+            turned = picked[...].T
+            cell = jnp.broadcast_to(cells_ref[pl.ds(b, 1), :], (recv, block_cells))
+            which = lax.rem(lax.div(cell, LANES), packed)
+            for level in range(levels):
+                value = turned[level * recv : (level + 1) * recv]
+                for q in range(1, packed):
+                    at = (q * levels + level) * recv
+                    value = jnp.where(which == q, turned[at : at + recv], value)
+                put(k, slice(level * block_cells, (level + 1) * block_cells), value)
+
+    def copy_to(j, i):
+        return pltpu.make_async_remote_copy(
+            src_ref=sending.at[j, i], dst_ref=landed.at[strip, batch],
+            send_sem=send_sem.at[j, i], recv_sem=recv_sem.at[j, i],
+            device_id=peer(j, i), device_id_type=MESH,
+        )
+
+    def sample(j, i):
+        def put(k, at, value):
+            sending[j, i, k, :, at] = value
+
+        pick(j, i, put)
+        copy_to(j, i).start()
+
+    pl.semaphore_wait(barrier, batches * strips - 1)
+
+    def sample_strip(j, _):
+        def one(i, _):
+            sample(j, i)
+            return 0
+
+        lax.fori_loop(0, batches, one, 0)
+        return 0
+
+    lax.fori_loop(1, strips, sample_strip, 0)
+
+    def sample_own_strip(i, _):
+        sample(0, i)
+        return 0
+
+    lax.fori_loop(1, batches, sample_own_strip, 0)
+
+    def put_own(k, at, value):
+        landed[strip, batch, k, :, at] = value
+
+    pick(0, 0, put_own)
+    profile_load.wait()
+
+    def contract(s):
+        for k in range(own):
+            left = landed[s, :, k].reshape(batches * recv, levels * block_cells)
+            out_ref[s, k] = jnp.dot(
+                left, profiles_ref[s, k], precision=lax.Precision.HIGHEST,
+                preferred_element_type=jnp.float32,
+            )
+
+    def receive(j, _):
+        for i in range(batches):
+            copy_to(j, i).wait_recv()
+        contract(lax.rem(strip + strips - j, strips))
+        return 0
+
+    lax.fori_loop(1, strips, receive, 0)
+    for i in range(1, batches):
+        copy_to(0, i).wait_recv()
+    contract(strip)
+
+    def sent(j, _):
+        for i in range(batches):
+            copy_to(j, i).wait_send()
+        return 0
+
+    lax.fori_loop(1, strips, sent, 0)
+    for i in range(1, batches):
+        copy_to(0, i).wait_send()
+
+
+def run_response(batches, strips, recv, levels, cells, by_cell, profiles):
+    blocks, block_cells = cells.shape
+    own = blocks // (batches * strips)
+    depth, scenarios = profiles.shape[-2:]
+    vmem = pl.BlockSpec(memory_space=pltpu.VMEM)
+    dma = pltpu.SemaphoreType.DMA
+    return pl.pallas_call(
+        functools.partial(response_kernel, batches, strips, recv, levels),
+        out_shape=jax.ShapeDtypeStruct((strips, own, batches * recv, scenarios), jnp.float32),
+        in_specs=[pl.BlockSpec(memory_space=pl.ANY)] * 3,
+        out_specs=vmem,
+        scratch_shapes=[
+            pltpu.VMEM(by_cell.shape, jnp.float32),
+            pltpu.VMEM(profiles.shape, jnp.float32),
+            pltpu.VMEM(cells.shape, jnp.int32),
             pltpu.VMEM(cells.shape, jnp.int32),
             pltpu.SMEM(cells.shape, jnp.int32),
-            pltpu.SemaphoreType.DMA,
-            pltpu.SemaphoreType.DMA,
-            pltpu.SemaphoreType.DMA,
-            pltpu.SemaphoreType.DMA((recv,)),
+            pltpu.VMEM((block_cells, LANES), jnp.float32),
+            pltpu.VMEM((strips, batches, own, recv, depth), jnp.float32),
+            pltpu.VMEM((strips, batches, own, recv, depth), jnp.float32),
+            dma,
+            dma,
+            dma((2,)),
+            dma((strips, batches)),
+            dma((strips, batches)),
         ],
-        compiler_params=pltpu.CompilerParams(vmem_limit_bytes=VMEM_LIMIT),
-        name="release_samples",
-    )(cells, field)
-
-
-def contract_kernel(samples_ref, profiles_ref, out_ref):
-    batches, own, recv, depth = samples_ref.shape
-    for b in range(own):
-        left = samples_ref[:, b].reshape(batches * recv, depth)
-        out_ref[b] = jnp.dot(
-            left, profiles_ref[b], precision=lax.Precision.HIGHEST,
-            preferred_element_type=jnp.float32,
-        )
-
-
-def run_contract(gathered, profiles):
-    batches, strips, own, recv, depth = gathered.shape
-    scenarios = profiles.shape[-1]
-    return pl.pallas_call(
-        contract_kernel,
-        grid=(strips,),
-        out_shape=jax.ShapeDtypeStruct((strips, own, batches * recv, scenarios), jnp.float32),
-        in_specs=[
-            pl.BlockSpec((batches, None, own, recv, depth), lambda s: (0, s, 0, 0, 0)),
-            pl.BlockSpec((None, own, depth, scenarios), lambda s: (s, 0, 0, 0)),
-        ],
-        out_specs=pl.BlockSpec((None, own, batches * recv, scenarios), lambda s: (s, 0, 0, 0)),
-        compiler_params=pltpu.CompilerParams(vmem_limit_bytes=VMEM_LIMIT),
-        name="scenario_response",
-    )(gathered, profiles)
+        compiler_params=pltpu.CompilerParams(
+            collective_id=1, has_side_effects=True, vmem_limit_bytes=VMEM_LIMIT
+        ),
+        name="release_response",
+    )(cells, by_cell, profiles)
 
 
 def on_device(
@@ -549,11 +656,12 @@
     stepped = run_steps(
         batches, strips, plan, decay, obs_weight, water_mask, mixing, adjoint_end, currents
     )
-    field, samples = run_samples(release_cells[0], stepped)
-    gathered = lax.all_to_all(samples, ("rcpt", "space"), split_axis=0, concat_axis=0, tiled=True)
-    own = samples.shape[0] // (batches * strips)
-    gathered = gathered.reshape((batches, strips, own) + samples.shape[1:])
-    return (field, run_contract(gathered, profiles))
+    field, by_cell = run_turn(stepped)
+    recv, levels = adjoint_end.shape[:2]
+    response = run_response(
+        batches, strips, recv, levels, release_cells[0], by_cell, profiles
+    )
+    return (field, response)
 
 
 def solution(mesh):

time: 83.7 us -> 70.8 us (0.85); the launches traced: 83.4 us -> 69.4 us
  blocking collectives: 22.5 us -> 0 us
  Pallas kernels: 55.3 us -> 67.2 us
  local copies, waits for them, and re-layouts: 4.93 us -> 1.57 us
    all_to_all x1 -> x0, blocking collectives: 22.5 us -> none  [on_device(): lax.all_to_all(samples, ('rcpt', 'space'), split_axis=0, concat_axis=0, t...]
    pallas_call x2, Pallas kernels: 14.4 us -> 25.3 us  [the longest x1 19 us: run_response(): pl.pallas_call(functools.partial(response_kernel, batches, strips, recv,...]
    unnamed x16 -> x1, local copies, waits for them, and re-layouts: 4.93 us -> 1.57 us
    pallas_call x1, Pallas kernels: 40.9 us -> 41.9 us  [run_steps(): pl.pallas_call(functools.partial(steps_kernel, batches, strips), out_shap...]
where the time goes in v3:
time: 70.8 us; the launch traced here: 69.4 us
  Pallas kernels  67.2 us (95%)
  local copies, waits for them, and re-layouts  1.57 us (2%)
    pallas_call x1, Pallas kernels, run_steps(): pl.pallas_call(functools.partial(steps_kernel, batches, strips), out_shap...  41.9 us
    pallas_call x1, Pallas kernels, run_response(): pl.pallas_call(functools.partial(response_kernel, batches, strips, recv,...  19 us
    pallas_call x1, Pallas kernels, run_turn(): pl.pallas_call(turn_kernel, out_shape=(jax.ShapeDtypeStruct((recv, levels...  6.27 us
    unnamed x1, local copies, waits for them, and re-layouts  1.57 us

profile of v3, /device:TPU:0, one launch (start us, length us, event | category | flops | bytes accessed | tf_op | source)
XLA Modules:
  0.0 69.4 jit_solution(18212773002924434170)
XLA Ops:
  0.6 41.9 %transport_steps.1.field_hbm = f32[4,32,8,1024]{3,2,1,0:T(8,128)} custom-call(s32[4]{0:T(128)} %plan_hbm.1, f32[8]{0:T(128)} %decay_hbm.1, f32[4,8]{1,0:T(4,128)} %obs_hbm.1, s32[32,1024]{1,0:T(8,128)} %water_hbm.1, f32[3,32,1024]{2,1,0:T(8,128)} %mix_hbm.1, f32[8,4,32,1024]{3,2,1,0:T(8,128)} %adj_hbm.1, bf16[1,2,4,32,1024]{4,3,2,1,0:T(8,128)(2,1)} %cur_hbm.1), custom_call_target="tpu_custom_call" | custom-call | tf_op jit(solution)/shard_map/transport_steps/pallas_call | solution.py:376
  42.5 6.3 %cell_major.1 = (f32[8,4,32,1024]{3,2,1,0:T(8,128)}, f32[8192,128]{1,0:T(8,128)}) custom-call(f32[4,32,8,1024]{3,2,1,0:T(8,128)} %transport_steps.1.field_hbm), custom_call_target="tpu_custom_call" | custom-call | tf_op jit(solution)/shard_map/cell_major/pallas_call | solution.py:472
  48.8 19.0 %release_response.1 = f32[8,1,32,128]{3,2,1,0:T(8,128)} custom-call(s32[32,128]{1,0:T(8,128)} %bitcast.1, f32[8192,128]{1,0:T(8,128)} %get-tuple-element.5.by_cell_hbm, f32[8,1,512,128]{3,2,1,0:T(8,128)} %profiles_hbm.1), custom_call_target="tpu_custom_call" | custom-call | tf_op jit(solution)/shard_map/release_response/pallas_call | solution.py:624
  67.8 1.6 %copy.12 = f32[8,1,32,128]{3,2,1,0:T(8,128)} copy(f32[8,1,32,128]{3,2,1,0:T(8,128)} %release_response.1) | data formatting | bytes 262144

commit v4 on v3

--- a/solution.py
+++ b/solution.py
@@ -10,6 +10,7 @@
 HOURS = 4
 LANES = 128
 SUBROWS = 16
+CHUNK = 256
 MESH = pl.DeviceIdType.MESH
 VMEM_LIMIT = 63 * 1024 * 1024
 
@@ -111,9 +112,8 @@
             ]
             for part in range(parts)
         ]
-    for copies in spread:
-        for copy in copies:
-            copy.start()
+    for copy in spread[0]:
+        copy.start()
 
     def pass_on(part):
         if square:
@@ -240,7 +240,7 @@
         value = jnp.zeros((recv, LANES), jnp.float32)
         for r in range(recv):
             value = jnp.where(sub == r, read(r), value)
-        return jnp.concatenate([value] * (width // LANES), 1)
+        return jnp.concatenate([value] * (min(CHUNK, width) // LANES), 1)
 
     keep = per_receptor(lambda r: 1.0 - decay_ref[r])
 
@@ -266,29 +266,57 @@
 
         lax.fori_loop(0, part_rows // SUBROWS, tile, 0)
 
-    def do_row(hour, fin, fout, i, upper, lower, obs):
-        at = pl.ds(i, 1)
-
-        def moved_at(level):
-            center = fin[level, i]
-            out = center * weight[hour, 0, level, at, :]
-            out = out + upper(level) * weight[hour, 1, level, at, :]
-            out = out + lower(level) * weight[hour, 2, level, at, :]
-            out = out + pltpu.roll(center, 1, 1) * weight[hour, 3, level, at, :]
-            return out + pltpu.roll(center, width - 1, 1) * weight[hour, 4, level, at, :]
-
-        moved = moved_at(0)
-        flux = None
-        for level in range(levels):
-            mixed = moved
-            if flux is not None:
-                mixed = mixed - flux
-            if level < levels - 1:
-                following = moved_at(level + 1)
-                flux = mix_ref[level, at, :] * (following - moved)
-                mixed = mixed + flux
-                moved = following
-            fout[level, i] = keep * mixed + obs * src[level, i]
+    chunk = min(CHUNK, width)
+
+    def do_rows(hour, fin, fout, i, count, upper, lower, obs):
+        for start in range(0, width, chunk):
+            cols = slice(start, start + chunk)
+
+            def beside(level, k, center):
+                if start > 0:
+                    wide = fin[level, i + k, :, start - LANES : start + chunk]
+                    before = pltpu.roll(wide, 1, 1)[:, LANES:]
+                else:
+                    before = pltpu.roll(center, 1, 1)
+                if start + chunk < width:
+                    wide = fin[level, i + k, :, start : start + chunk + LANES]
+                    after = pltpu.roll(wide, chunk + LANES - 1, 1)[:, :chunk]
+                else:
+                    after = pltpu.roll(center, chunk - 1, 1)
+                return before, after
+
+            def moved_at(level):
+                lines = [upper(level, cols)]
+                lines += [fin[level, i + k, :, cols] for k in range(count)]
+                lines += [lower(level, cols)]
+                found = []
+                for k in range(count):
+                    center = lines[k + 1]
+                    before, after = beside(level, k, center)
+                    factor = [weight[hour, n, level, pl.ds(i + k, 1), cols] for n in range(5)]
+                    out = center * factor[0] + lines[k] * factor[1]
+                    out = out + lines[k + 2] * factor[2]
+                    found.append(out + before * factor[3] + after * factor[4])
+                return found
+
+            moved = moved_at(0)
+            flux = None
+            for level in range(levels):
+                mixed = moved
+                if flux is not None:
+                    mixed = [m - f for m, f in zip(mixed, flux)]
+                if level < levels - 1:
+                    following = moved_at(level + 1)
+                    flux = [
+                        mix_ref[level, pl.ds(i + k, 1), cols] * (following[k] - moved[k])
+                        for k in range(count)
+                    ]
+                    mixed = [m + f for m, f in zip(mixed, flux)]
+                    moved = following
+                for k in range(count):
+                    fout[level, i + k, :, cols] = (
+                        keep * mixed[k] + obs * src[level, i + k, :, cols]
+                    )
 
     seen = [per_receptor(lambda r, h=h: obs_ref[h, r]) for h in range(HOURS)]
 
@@ -299,35 +327,49 @@
         hour = HOURS - 1 - step
         fin, fout = buffers(step)
 
-        def body(i, _):
-            do_row(
-                hour, fin, fout, i,
-                lambda level: fin[level, i - 1], lambda level: fin[level, i + 1], seen[hour],
+        def some(i, count):
+            do_rows(
+                hour, fin, fout, i, count,
+                lambda level, cols: fin[level, i - 1, :, cols],
+                lambda level, cols: fin[level, i + count, :, cols],
+                seen[hour],
             )
+
+        def body(t, _):
+            some(low + 2 * t, 2)
             return 0
 
-        if low < high:
-            lax.fori_loop(low, high, body, 0)
+        if high - low > 1:
+            lax.fori_loop(0, (high - low) // 2, body, 0)
+        if low < high and (high - low) % 2:
+            some(high - 1, 1)
 
     def first_row(step):
         hour = HOURS - 1 - step
         fin, fout = buffers(step)
-        do_row(
-            hour, fin, fout, 0,
-            lambda level: halo[step, 0, level], lambda level: fin[level, 1], seen[hour],
+        do_rows(
+            hour, fin, fout, 0, 1,
+            lambda level, cols: halo[step, 0, level, :, cols],
+            lambda level, cols: fin[level, 1, :, cols],
+            seen[hour],
         )
 
     def last_row(step):
         hour = HOURS - 1 - step
         fin, fout = buffers(step)
-        do_row(
-            hour, fin, fout, rows - 1,
-            lambda level: fin[level, rows - 2], lambda level: halo[step, 1, level], seen[hour],
+        do_rows(
+            hour, fin, fout, rows - 1, 1,
+            lambda level, cols: fin[level, rows - 2, :, cols],
+            lambda level, cols: halo[step, 1, level, :, cols],
+            seen[hour],
         )
 
     for copy in own_copies:
         copy.wait()
     pass_on(0)
+    for copies in spread[1:]:
+        for copy in copies:
+            copy.start()
     for part in range(parts):
         arrived(part)
         if part < parts - 1:

time: 70.8 us -> 69.3 us (0.979)
  Pallas kernels: 67.2 us -> 66 us
    pallas_call x1, Pallas kernels: 41.9 us -> 39.5 us  [run_steps(): pl.pallas_call(functools.partial(steps_kernel, batches, strips), out_shap...]
    pallas_call x1, Pallas kernels: 19 us -> 20.2 us  [run_response(): pl.pallas_call(functools.partial(response_kernel, batches, strips, recv,...]
where the time goes in v4:
time: 69.3 us; the launch traced here: 68.2 us
  Pallas kernels  66 us (95%)
  local copies, waits for them, and re-layouts  1.57 us (2%)
    pallas_call x1, Pallas kernels, run_steps(): pl.pallas_call(functools.partial(steps_kernel, batches, strips), out_shap...  39.5 us
    pallas_call x1, Pallas kernels, run_response(): pl.pallas_call(functools.partial(response_kernel, batches, strips, recv,...  20.2 us
    pallas_call x1, Pallas kernels, run_turn(): pl.pallas_call(turn_kernel, out_shape=(jax.ShapeDtypeStruct((recv, levels...  6.27 us
    unnamed x1, local copies, waits for them, and re-layouts  1.57 us

profile of v4, /device:TPU:0, one launch (start us, length us, event | category | flops | bytes accessed | tf_op | source)
XLA Modules:
  0.0 68.2 jit_solution(6655829855973627926)
XLA Ops:
  0.6 39.5 %transport_steps.1.field_hbm = f32[4,32,8,1024]{3,2,1,0:T(8,128)} custom-call(s32[4]{0:T(128)} %plan_hbm.1, f32[8]{0:T(128)} %decay_hbm.1, f32[4,8]{1,0:T(4,128)} %obs_hbm.1, s32[32,1024]{1,0:T(8,128)} %water_hbm.1, f32[3,32,1024]{2,1,0:T(8,128)} %mix_hbm.1, f32[8,4,32,1024]{3,2,1,0:T(8,128)} %adj_hbm.1, bf16[1,2,4,32,1024]{4,3,2,1,0:T(8,128)(2,1)} %cur_hbm.1), custom_call_target="tpu_custom_call" | custom-call | tf_op jit(solution)/shard_map/transport_steps/pallas_call | solution.py:418
  40.1 6.3 %cell_major.1 = (f32[8,4,32,1024]{3,2,1,0:T(8,128)}, f32[8192,128]{1,0:T(8,128)}) custom-call(f32[4,32,8,1024]{3,2,1,0:T(8,128)} %transport_steps.1.field_hbm), custom_call_target="tpu_custom_call" | custom-call | tf_op jit(solution)/shard_map/cell_major/pallas_call | solution.py:514
  46.4 20.2 %release_response.1 = f32[8,1,32,128]{3,2,1,0:T(8,128)} custom-call(s32[32,128]{1,0:T(8,128)} %bitcast.1, f32[8192,128]{1,0:T(8,128)} %get-tuple-element.5.by_cell_hbm, f32[8,1,512,128]{3,2,1,0:T(8,128)} %profiles_hbm.1), custom_call_target="tpu_custom_call" | custom-call | tf_op jit(solution)/shard_map/release_response/pallas_call | solution.py:666
  66.6 1.6 %copy.12 = f32[8,1,32,128]{3,2,1,0:T(8,128)} copy(f32[8,1,32,128]{3,2,1,0:T(8,128)} %release_response.1) | data formatting | bytes 262144
